TPU v7x, 32 devices: a whole 2x2x4 slice. The times are simulated.
32 devices in a mesh: freq: 8 (over z, y), tile: 4 (over x, core).
Axes of the slice: x: 2, y: 2, z: 4, core: 2. Of those that a mesh axis runs over, the one named last changes fastest.
Arguments:
- voltages: bfloat16 [1024, 262912], P(('tile', 'freq')), may hold values from -8 to 8
- gain_re: float32 [1024, 128], P(('tile', 'freq')), may hold values from -3 to 3
- gain_im: float32 [1024, 128], P(('tile', 'freq')), may hold values from -3 to 3
Outputs:
- visibility: float32 [2, 128, 1024, 1024], P(None, 'freq', 'tile')
All inputs are finite; a program needn't handle non-finite values.
Results may differ from a plain program's by a relative error of at most 0.0013.
Values may be sent and summed in bfloat16 or wider, within the bound.
No kernel may reach another device: no remote copies, remote signals or barrier semaphores. Data moves between devices by JAX's collectives and lax.ppermute only.
A program may use at most 384 MiB of HBM per device.

v0:
```python
import jax
import jax.numpy as jnp
from jax import lax
from jax.sharding import PartitionSpec as P

NFFT = 256
TAPS = 4
CH = 128
FRAMES = 1024
FIRST = 0


def window_table(tap_count, length):
    count = tap_count * length
    sample_idx = jnp.arange(count).astype(jnp.float32)
    center = (count - 1) / 2.0
    shaped = jnp.sinc((sample_idx - center) / length) * (
        0.5 - 0.5 * jnp.cos(2.0 * jnp.pi * sample_idx / (count - 1))
    )
    return shaped.reshape(tap_count, length)


def fourier_table(length, channels, lowest):
    sample_idx = jnp.arange(length, dtype=jnp.int32)
    channel_idx = jnp.arange(channels, dtype=jnp.int32) + lowest
    product = sample_idx[:, None] * channel_idx[None, :] % length
    angle = 2.0 * jnp.pi * product.astype(jnp.float32) / length
    factor = 1.0 / jnp.sqrt(jnp.float32(length))
    return jnp.concatenate([jnp.cos(angle) * factor, -jnp.sin(angle) * factor], axis=1).astype(
        jnp.bfloat16
    )


def correlate(row_data, col_data, factor):
    products = jnp.einsum(
        "pcif,qcjf->pqcij", row_data, col_data, preferred_element_type=jnp.float32
    )
    real_part = products[0, 0] + products[1, 1]
    imag_part = products[1, 0] - products[0, 1]
    return jnp.stack([real_part, imag_part]) * factor


def per_device(voltages, gain_re, gain_im):
    frames = FRAMES
    tap_count = TAPS
    length = NFFT
    owned = voltages.shape[0]
    blocks = voltages.reshape(owned, frames + tap_count - 1, length)
    window = window_table(tap_count, length)
    filtered = window[0][None, None, :] * blocks[:, 0:frames, :].astype(jnp.float32)
    for tap_index in range(1, tap_count):
        filtered = filtered + window[tap_index][None, None, :] * blocks[
            :, tap_index : tap_index + frames, :
        ].astype(jnp.float32)
    filtered = filtered.astype(jnp.bfloat16)
    unscaled = jnp.einsum(
        "ifn,nc->cif",
        filtered,
        fourier_table(length, CH, FIRST),
        preferred_element_type=jnp.float32,
    )
    channels = unscaled.shape[0] // 2
    spec_re = unscaled[:channels]
    spec_im = unscaled[channels:]
    weight_re = gain_re.T[:, :, None]
    weight_im = gain_im.T[:, :, None]
    spectra = jnp.stack(
        [weight_re * spec_re - weight_im * spec_im, weight_re * spec_im + weight_im * spec_re]
    ).astype(jnp.bfloat16)
    turned = lax.all_to_all(spectra, "freq", split_axis=1, concat_axis=2, tiled=True)
    factor = 1.0 / frames
    return correlate(turned, lax.all_gather(turned, "tile", axis=2, tiled=True), factor)


def solution(mesh):
    in_specs = (P(("tile", "freq"), None), P(("tile", "freq"), None), P(("tile", "freq"), None))
    out_specs = P(None, "freq", "tile", None)
    return jax.shard_map(
        per_device, mesh=mesh, in_specs=in_specs, out_specs=out_specs, check_vma=False
    )
```

profile of v0, /device:TPU:0, one launch (start us, length us, event | category | flops | bytes accessed | tf_op | source)
XLA Modules:
  0.0 1028.8 jit_solution(12674323062497386649)
XLA Ops:
  6.5 0.0 all-gather.2.cloned.1.call-start
  6.6 0.5 multiply_convert_fusion
  7.1 24.3 %reshape.54 = bf16[32,1027,256]{2,1,0:T(8,128)(2,1)} reshape(bf16[32,262912]{1,0:T(8,128)(2,1)} %param.3) | data formatting | bytes 33652736 | tf_op jit(solution)/shard_map/reshape | solution.py:48
  31.4 0.0 copy-start
  31.4 0.0 copy-start.1
  31.4 42.7 %fusion.5 = f32[256,32,1024]{2,0,1:T(8,128)} fusion(bf16[32,1027,256]{2,1,0:T(8,128)(2,1)} %reshape.54, f32[256]{0:T(256)S(1)} %get-tuple-element.8, f32[256]{0:T(256)S(1)} %get-tuple-element.9, f32[256]{0:T(256)S(1)} %get-tuple-element.10, f32[256]{0:T(256)S(1)} %get-tuple-element.7, bf16[256,128]{0,1:T(8,128)(2,1)S(1)} %get-tuple-element.11, ...), kind=kOutput, calls=%fused_computation.5 | convolution fusion | flops 4395892736 | bytes 100798464 | tf_op jit(solution)/shard_map/ifn,nc->cif/dot_general | solution.py:56
  74.1 0.0 copy-done
  74.1 0.0 copy-done.1
  74.1 12.0 %fusion.17 = (bf16[1,128,32,1024]{3,1,2,0:T(8,128)(2,1)S(1)}, bf16[1,128,32,1024]{3,1,2,0:T(8,128)(2,1)S(1)}) fusion(f32[256,32,1024]{2,0,1:T(8,128)} %fusion.5, f32[128,32]{0,1:T(8,128)S(1)} %bitcast.44, f32[128,32]{0,1:T(8,128)S(1)} %bitcast.45), kind=kLoop, calls=%fused_computation.23 | loop fusion | flops 33554432 | bytes 50364416 | tf_op jit(solution)/shard_map/stack | solution.py:67
  86.1 1.7 pad_maximum_fusion
  87.7 21.8 %copy.12 = bf16[2,128,32,1024]{3,2,0,1:T(8,128)(2,1)S(1)} copy(bf16[2,128,32,1024]{3,1,2,0:T(8,128)(2,1)S(1)} %pad_maximum_fusion) | data formatting | bytes 33554432 | tf_op jit(solution)/shard_map/stack | solution.py:67
  109.5 369.9 %all_to_all.18 = bf16[2,128,32,1024]{3,2,0,1:T(8,128)(2,1)S(1)} all-to-all(bf16[2,128,32,1024]{3,2,0,1:T(8,128)(2,1)S(1)} %copy.12), channel_id=1, replica_groups=mesh['freq'=8,'tile'=4] {'freq'}, dimensions={1} | all-to-all | bytes 33554432 | tf_op jit(solution)/shard_map/all_to_all | solution.py:70
  479.5 6.7 copy.13
  486.1 0.0 all-gather.2.cloned.1.call-update
  486.1 391.9 %all-gather.2.cloned.1.call-done = bf16[2,16,1024,1024]{3,2,0,1:T(8,128)(2,1)} async-done(((bf16[2,16,256,1024]{3,2,0,1:T(8,128)(2,1)}), bf16[2,16,1024,1024]{3,2,0,1:T(8,128)(2,1)}) %all-gather.2.cloned.1.call-update) | async-done | bytes 67108880 | tf_op jit(solution)/shard_map/all_gather | solution.py:72
  878.0 62.4 %fusion.2 = f32[2,2,16,256,1024]{3,4,0,1,2:T(8,128)} fusion(bf16[2,16,256,1024,1]{3,2,0,4,1:T(8,128)(2,1)} %bitcast.42, bf16[2,16,1024,1024]{3,2,0,1:T(8,128)(2,1)} %all-gather.2.cloned.1.call-done), kind=kOutput, calls=%fused_computation.4 | convolution fusion | flops 34359738368 | bytes 150994944 | tf_op jit(solution)/shard_map/pcif,qcjf->pqcij/dot_general | solution.py:35
  940.4 11.4 %fusion.6 = f32[1,16,256,1024]{2,3,1,0:T(8,128)S(1)} fusion(f32[2,2,16,256,1024]{3,4,0,1,2:T(8,128)} %fusion.2), kind=kLoop, calls=%fused_computation.7 | loop fusion | flops 4194304 | bytes 50331648 | tf_op jit(solution)/shard_map/sub | solution.py:39
  951.9 17.9 %fusion.8 = f32[1,16,256,1024]{2,3,1,0:T(8,128)} fusion(f32[2,2,16,256,1024]{3,4,0,1,2:T(8,128)} %fusion.2), kind=kLoop, calls=%fused_computation.10 | loop fusion | flops 4194304 | bytes 50331648 | tf_op jit(solution)/shard_map/add | solution.py:38
  969.8 18.6 %maximum_multiply_fusion = f32[2,16,256,1024]{2,3,1,0:T(8,128)} fusion(f32[1,16,256,1024]{2,3,1,0:T(8,128)S(1)} %fusion.6, f32[1,16,256,1024]{2,3,1,0:T(8,128)} %fusion.8), kind=kLoop, calls=%fused_computation.2 | loop fusion | flops 16777216 | bytes 67108864 | tf_op jit(solution)/shard_map/mul | solution.py:40
  988.4 33.6 %copy.16 = f32[2,16,256,1024]{3,2,1,0:T(8,128)} copy(f32[2,16,256,1024]{2,3,1,0:T(8,128)} %maximum_multiply_fusion) | data formatting | bytes 67108864 | tf_op jit(solution)/shard_map/mul | solution.py:40
  (2 shorter events, 0.1 us)
Async XLA Ops:
  6.5 871.5 %all-gather.2.cloned.1.call-start = ((), (), s32[]{:S(2)}) async-start(), calls=%async_computation.1 | async-start | bytes 83886080 | tf_op jit(solution)/shard_map/all_gather | solution.py:72
  31.4 42.7 %copy-start = (f32[32,128]{1,0:T(8,128)S(1)}, f32[32,128]{1,0:T(8,128)}, u32[]{:S(2)}) copy-start(f32[32,128]{1,0:T(8,128)} %param.5) | copy-start | bytes 49156
  31.4 42.7 %copy-start.1 = (f32[32,128]{1,0:T(8,128)S(1)}, f32[32,128]{1,0:T(8,128)}, u32[]{:S(2)}) copy-start(f32[32,128]{1,0:T(8,128)} %param.4) | copy-start | bytes 49156
Sparse Core Ops, SparseCore 0:
  486.3 391.7 all-gather.1
where the time goes:
time: 1030 us
  waiting for transfers between devices  392 us (38%)
  blocking collectives  370 us (36%)
  matrix products  105 us (10%)
  local copies, waits for them, and re-layouts  86.3 us (8%)
  other arithmetic  62.2 us (6%)
  between operations  13.4 us (1%)
    all_gather x1, waiting for transfers between devices, per_device(): lax.all_gather(turned, 'tile', axis=2, tiled=True)  392 us
    all_to_all x1, blocking collectives, per_device(): lax.all_to_all(spectra, 'freq', split_axis=1, concat_axis=2, tiled=True)  370 us
    dot_general x1, matrix products, correlate(): jnp.einsum('pcif,qcjf->pqcij', row_data, col_data, preferred_element_type...  62.4 us
    dot_general x1, matrix products, per_device(): jnp.einsum('ifn,nc->cif', filtered, fourier_table(length, CH, FIRST), pre...  42.7 us
    mul x1, local copies, waits for them, and re-layouts, correlate(): return jnp.stack([real_part, imag_part]) * factor  33.6 us
    reshape x1, local copies, waits for them, and re-layouts, per_device(): blocks = voltages.reshape(owned, frames + tap_count - 1, length)  24.3 us
    another operation x1, local copies, waits for them, and re-layouts, per_device(): jnp.stack([weight_re * spec_re - weight_im * spec_im, weight_re * spec_im...  21.8 us
  transfers between devices with their start and end apart: 1, of which 1 were waited for; matrix products, arithmetic and copies ran while one was open for 0% of the time, Pallas kernels for 0%

commit v1 on v0

v1 whole, which is shorter than its diff:
```python
import functools

import jax
import jax.numpy as jnp
from jax import lax
from jax.experimental import pallas as pl
from jax.experimental.pallas import tpu as pltpu
from jax.sharding import PartitionSpec as P

NFFT = 256
TAPS = 4
CH = 128
FRAMES = 1024
FIRST = 0
LANES = 128
VMEM = 60 * 1024 * 1024


def window_table(tap_count, length):
    count = tap_count * length
    sample_idx = jnp.arange(count).astype(jnp.float32)
    center = (count - 1) / 2.0
    shaped = jnp.sinc((sample_idx - center) / length) * (
        0.5 - 0.5 * jnp.cos(2.0 * jnp.pi * sample_idx / (count - 1))
    )
    return shaped.reshape(tap_count, length)


def fourier_table(length, channels, lowest):
    sample_idx = jnp.arange(length, dtype=jnp.int32)
    channel_idx = jnp.arange(channels, dtype=jnp.int32) + lowest
    product = sample_idx[:, None] * channel_idx[None, :] % length
    angle = 2.0 * jnp.pi * product.astype(jnp.float32) / length
    factor = 1.0 / jnp.sqrt(jnp.float32(length))
    return jnp.concatenate([jnp.cos(angle) * factor, -jnp.sin(angle) * factor], axis=1).astype(
        jnp.bfloat16
    )


def chunk_sizes(channels):
    if channels == 16:
        return (2, 2, 2, 2, 2, 2, 2, 2)
    return (1,) * channels


def analyse_kernel(
    owned, freq, sizes, volt_ref, h0_ref, h1_ref, h2_ref, window_ref, table_ref, gre_ref, gim_ref, *rest
):
    outs, (low_ref, high_ref, spec_ref) = rest[: len(sizes)], rest[len(sizes) :]
    halos = (h0_ref, h1_ref, h2_ref)

    def tap(position):
        if isinstance(position, int) and position >= LANES:
            return halos[position - LANES][...].astype(jnp.float32)
        return volt_ref[:, pl.ds(pl.multiple_of(position * NFFT, NFFT), NFFT)].astype(jnp.float32)

    def filter_at(position, store):
        total = window_ref[0:1, :] * tap(position)
        for p in range(1, TAPS):
            total = total + window_ref[p : p + 1, :] * tap(position + p)
        at = pl.ds(pl.multiple_of(store * owned, owned), owned)
        low_ref[at, :] = total[:, :LANES]
        high_ref[at, :] = total[:, LANES:]

    group = 4

    def step(g, carry):
        base = g * group
        for u in range(group):
            filter_at(base + u, base + u)
        return carry

    lax.fori_loop(0, LANES // group - 1, step, 0)
    for position in range(LANES - group, LANES):
        filter_at(position, position)

    pair = 2

    def transform(g, carry):
        rows = jnp.concatenate(
            [
                jnp.concatenate(
                    [ref[pl.ds(g * pair + u, LANES, stride=owned), :] for ref in (low_ref, high_ref)],
                    axis=1,
                )
                for u in range(pair)
            ],
            axis=0,
        ).astype(jnp.bfloat16)
        result = lax.dot_general(
            table_ref[...], rows, (((1,), (1,)), ((), ())), preferred_element_type=jnp.float32
        )
        for u in range(pair):
            spec_ref[pl.ds(g * pair + u, 2 * CH, stride=owned), :] = result[
                :, u * LANES : (u + 1) * LANES
            ]
        return carry

    lax.fori_loop(0, owned // pair, transform, 0)

    channels = CH // freq
    start = 0
    for k, size in enumerate(sizes):
        for u in range(size):

            def finish(dest, carry, k=k, u=u, place=start + u):
                channel = dest * channels + place
                at = pl.ds(pl.multiple_of(channel * owned, owned), owned)
                im_at = pl.ds(pl.multiple_of((CH + channel) * owned, owned), owned)
                re, im = spec_ref[at, :], spec_ref[im_at, :]
                gre, gim = gre_ref[at, :], gim_ref[at, :]
                outs[k][dest, u, 0] = (gre * re - gim * im).astype(jnp.bfloat16)
                outs[k][dest, u, 1] = (gre * im + gim * re).astype(jnp.bfloat16)
                return carry

            lax.fori_loop(0, freq, finish, 0, unroll=min(freq, 8))
        start += size


def analyse(voltages, gain_re, gain_im, freq, sizes):
    owned = voltages.shape[0]
    span = LANES * NFFT
    table = fourier_table(NFFT, CH, FIRST).T
    window = window_table(TAPS, NFFT)

    def spread(gain):
        return jnp.broadcast_to(gain.T[:, :, None], (CH, owned, LANES)).reshape(CH * owned, LANES)

    halo = [
        pl.BlockSpec((owned, NFFT), lambda b, q=q: (0, (b + 1) * LANES + q)) for q in range(TAPS - 1)
    ]
    whole = lambda shape: pl.BlockSpec(shape, lambda b: (0, 0))
    return pl.pallas_call(
        functools.partial(analyse_kernel, owned, freq, sizes),
        grid=(FRAMES // LANES,),
        in_specs=[
            pl.BlockSpec((owned, span), lambda b: (0, b)),
            *halo,
            whole((TAPS, NFFT)),
            whole((2 * CH, NFFT)),
            whole((CH * owned, LANES)),
            whole((CH * owned, LANES)),
        ],
        out_specs=[
            pl.BlockSpec((freq, size, 2, owned, LANES), lambda b: (0, 0, 0, 0, b)) for size in sizes
        ],
        out_shape=[
            jax.ShapeDtypeStruct((freq, size, 2, owned, FRAMES), jnp.bfloat16) for size in sizes
        ],
        scratch_shapes=[
            pltpu.VMEM((LANES * owned, LANES), jnp.float32),
            pltpu.VMEM((LANES * owned, LANES), jnp.float32),
            pltpu.VMEM((2 * CH * owned, LANES), jnp.float32),
        ],
        compiler_params=pltpu.CompilerParams(vmem_limit_bytes=VMEM),
        cost_estimate=pl.CostEstimate(
            flops=2 * owned * FRAMES * NFFT * 2 * CH, bytes_accessed=4 * voltages.size, transcendentals=0
        ),
    )(voltages, voltages, voltages, voltages, window, table, spread(gain_re), spread(gain_im))


def correlate_kernel(tiles, me_ref, *rest):
    blocks, out_ref, left_ref = rest[:tiles], rest[-2], rest[-1]
    own = blocks[0]
    rows = own.shape[0] * own.shape[3]
    re = own[:, 0, 0].reshape(rows, FRAMES)
    im = own[:, 0, 1].reshape(rows, FRAMES)
    left_ref[0:rows, 0:FRAMES] = re
    left_ref[0:rows, FRAMES:] = im
    left_ref[rows:, 0:FRAMES] = im
    left_ref[rows:, FRAMES:] = -re
    factor = 1.0 / FRAMES
    for r in range(tiles):
        other = jnp.concatenate(
            [blocks[r][:, 0, 0].reshape(rows, FRAMES), blocks[r][:, 0, 1].reshape(rows, FRAMES)], axis=1
        )
        both = lax.dot_general(
            left_ref[...], other, (((1,), (1,)), ((), ())), preferred_element_type=jnp.float32
        )
        at = pl.ds(pl.multiple_of((me_ref[0] ^ r) * rows, rows), rows)
        out_ref[0, 0, :, at] = both[:rows] * factor
        out_ref[1, 0, :, at] = both[rows:] * factor


def correlate(me, blocks, previous, first, channels):
    freq, size, _, owned, frames = blocks[0].shape
    tiles = len(blocks)
    rows = freq * owned
    in_specs = [
        pl.BlockSpec((freq, 1, 2, owned, frames), lambda c, me: (0, c, 0, 0, 0)) for _ in blocks
    ]
    args = [me, *blocks]
    aliases = {}
    if previous is not None:
        in_specs.append(pl.BlockSpec(memory_space=pl.ANY))
        aliases = {len(args): 0}
        args.append(previous)
    return pl.pallas_call(
        functools.partial(correlate_kernel, tiles),
        grid_spec=pltpu.PrefetchScalarGridSpec(
            num_scalar_prefetch=1,
            grid=(size,),
            in_specs=in_specs,
            out_specs=pl.BlockSpec((2, 1, rows, tiles * rows), lambda c, me: (0, first + c, 0, 0)),
            scratch_shapes=[pltpu.VMEM((2 * rows, 2 * frames), jnp.bfloat16)],
        ),
        out_shape=jax.ShapeDtypeStruct((2, channels, rows, tiles * rows), jnp.float32),
        input_output_aliases=aliases,
        compiler_params=pltpu.CompilerParams(vmem_limit_bytes=VMEM),
        cost_estimate=pl.CostEstimate(
            flops=size * 2 * (2 * rows) * (2 * frames) * (tiles * rows),
            bytes_accessed=size * (tiles * rows * frames * 4 + 2 * rows * tiles * rows * 4),
            transcendentals=0,
        ),
    )(*args)


def per_device(freq, tile, voltages, gain_re, gain_im):
    channels = CH // freq
    sizes = chunk_sizes(channels)
    me = lax.axis_index("tile").astype(jnp.int32).reshape(1)
    messages = list(analyse(voltages, gain_re, gain_im, freq, sizes))

    def swap(array, bit):
        return lax.ppermute(array, "tile", [(t, t ^ bit) for t in range(tile)])

    count = len(sizes)
    firsts = [sum(sizes[:k]) for k in range(count)]
    turned, across, beside, opposite = ([None] * count for _ in range(4))
    result = None

    def finish(k):
        blocks = [turned[k], beside[k], across[k], opposite[k]]
        return correlate(me, blocks, result, firsts[k], channels)

    for k in range(count):
        message = messages[k]
        if k >= 2:
            message, across[k - 2] = lax.optimization_barrier((message, across[k - 2]))
            opposite[k - 2] = swap(across[k - 2], 1)
        if k >= 3:
            message, opposite[k - 3], beside[k - 3] = lax.optimization_barrier(
                (message, opposite[k - 3], beside[k - 3])
            )
            if k >= 4:
                message, result = lax.optimization_barrier((message, result))
            result = finish(k - 3)
        turned[k] = lax.all_to_all(message, "freq", split_axis=0, concat_axis=0, tiled=True)
        across[k] = swap(turned[k], 2)
        beside[k] = swap(turned[k], 1)
    for k in range(count - 2, count):
        opposite[k] = swap(across[k], 1)
    for k in range(count - 3, count):
        result = finish(k)
    return result


def solution(mesh):
    in_specs = (P(("tile", "freq"), None), P(("tile", "freq"), None), P(("tile", "freq"), None))
    out_specs = P(None, "freq", "tile", None)
    return jax.shard_map(
        functools.partial(per_device, mesh.shape["freq"], mesh.shape["tile"]),
        mesh=mesh,
        in_specs=in_specs,
        out_specs=out_specs,
        check_vma=False,
    )
```

time: 1030 us -> 608 us (0.59)
  blocking collectives: 370 us -> 55.6 us
  Pallas kernels: 0 us -> 163 us
  matrix products: 105 us -> 0 us
  local copies, waits for them, and re-layouts: 86.3 us -> 13.7 us
  waiting for transfers between devices: 392 us -> 323 us
  other arithmetic: 62.2 us -> 1.87 us
  starting transfers between devices: 0.01 us -> 49.6 us
  between operations: 13.4 us -> 0.07 us
    all_gather x1 -> x0, waiting for transfers between devices: 392 us -> none  [per_device(): lax.all_gather(turned, 'tile', axis=2, tiled=True)]
    all_to_all x1, blocking collectives: 370 us -> 55.6 us  [per_device(): lax.all_to_all(message, 'freq', split_axis=0, concat_axis=0, tiled=True)]
    ppermute x0 -> x24, waiting for transfers between devices: none -> 273 us  [swap(): return lax.ppermute(array, 'tile', [(t, t ^ bit) for t in range(tile)])]
    pallas_call x0 -> x9, Pallas kernels: none -> 163 us  [the longest x1 95.4 us: analyse(): pl.pallas_call(functools.partial(analyse_kernel, owned, freq, sizes), gri...]
    dot_general x2 -> x0, matrix products: 105 us -> none  [the longest x1 62.4 us: correlate(): jnp.einsum('pcif,qcjf->pqcij', row_data, col_data, preferred_element_type...]
    all_to_all x0 -> x7, waiting for transfers between devices: none -> 49.7 us  [per_device(): lax.all_to_all(message, 'freq', split_axis=0, concat_axis=0, tiled=True)]
    all_to_all x0 -> x7, starting transfers between devices: none -> 34 us  [per_device(): lax.all_to_all(message, 'freq', split_axis=0, concat_axis=0, tiled=True)]
    mul x1 -> x0, local copies, waits for them, and re-layouts: 33.6 us -> none  [correlate(): return jnp.stack([real_part, imag_part]) * factor]
  transfers between devices with their start and end apart: 1 -> 31, of which waited for: 1 -> 12; matrix products, arithmetic and copies ran while one was open for 0% -> 0% of each run, Pallas kernels for 0% -> 10%
where the time goes in v1:
time: 608 us; the launch traced here: 607 us
  waiting for transfers between devices  323 us (53%)
  Pallas kernels  163 us (27%)
  blocking collectives  55.6 us (9%)
  starting transfers between devices  49.6 us (8%)
  local copies, waits for them, and re-layouts  13.7 us (2%)
    ppermute x24, waiting for transfers between devices, swap(): return lax.ppermute(array, 'tile', [(t, t ^ bit) for t in range(tile)])  273 us
    pallas_call x1, Pallas kernels, analyse(): pl.pallas_call(functools.partial(analyse_kernel, owned, freq, sizes), gri...  95.4 us
    pallas_call x8, Pallas kernels, correlate(): pl.pallas_call(functools.partial(correlate_kernel, tiles), grid_spec=pltp...  67.6 us
    all_to_all x1, blocking collectives, per_device(): lax.all_to_all(message, 'freq', split_axis=0, concat_axis=0, tiled=True)  55.6 us
    all_to_all x7, waiting for transfers between devices, per_device(): lax.all_to_all(message, 'freq', split_axis=0, concat_axis=0, tiled=True)  49.7 us
    all_to_all x7, starting transfers between devices, per_device(): lax.all_to_all(message, 'freq', split_axis=0, concat_axis=0, tiled=True)  34 us
    ppermute x24, starting transfers between devices, swap(): return lax.ppermute(array, 'tile', [(t, t ^ bit) for t in range(tile)])  15.6 us
  transfers between devices with their start and end apart: 31, of which 12 were waited for; matrix products, arithmetic and copies ran while one was open for 0% of the time, Pallas kernels for 10%

profile of v1, /device:TPU:0, one launch (start us, length us, event | category | flops | bytes accessed | tf_op | source)
XLA Modules:
  0.0 606.7 jit_solution(151571021356440310)
XLA Ops:
  7.5 95.4 %shard_map.37 = (bf16[8,2,2,32,1024]{4,3,2,1,0:T(8,128)(2,1)}, bf16[8,2,2,32,1024]{4,3,2,1,0:T(8,128)(2,1)}, bf16[8,2,2,32,1024]{4,3,2,1,0:T(8,128)(2,1)}, bf16[...) custom-call(bf16[32,262912]{1,0:T(8,128)(2,1)} %h2_ref.1, ...), custom_call_target="tpu_custom_call" | custom-call | flops 4294967296 | bytes 33652736 | tf_op jit(solution)/shard_map/pallas_call | solution.py:133
  102.9 55.6 %all_to_all.40.rest_0_ = bf16[8,2,2,32,1024]{4,3,2,1,0:T(8,128)(2,1)} all-to-all(bf16[8,2,2,32,1024]{4,3,2,1,0:T(8,128)(2,1)} %get-tuple-element.54), channel_id=1, replica_groups=mesh['freq'=8,'tile'=4] {'freq'}, dimensions={0} | all-to-all | bytes 4194304 | tf_op jit(solution)/shard_map/all_to_all | solution.py:248
  163.7 45.4 %collective-permute-done.1.rest_2_ = bf16[8,2,2,32,1024]{4,3,2,1,0:T(8,128)(2,1)S(1)} collective-permute-done((bf16[8,2,2,32,1024]{4,3,2,1,0:T(8,128)(2,1)}, bf16[8,2,2,32,1024]{4,3,2,1,0:T(8,128)(2,1)S(1)}, u32[]{:S(2)}, u32[]{:S(2)}) %collective-permute-start.1) | collective-permute-done | bytes 2097184 | tf_op jit(solution)/shard_map/ppermute | solution.py:225
  211.8 5.7 all-to-all-start.3
  219.6 43.5 %collective-permute-done.rest_2_ = bf16[8,2,2,32,1024]{4,3,2,1,0:T(8,128)(2,1)S(1)} collective-permute-done((bf16[8,2,2,32,1024]{4,3,2,1,0:T(8,128)(2,1)}, bf16[8,2,2,32,1024]{4,3,2,1,0:T(8,128)(2,1)S(1)}, u32[]{:S(2)}, u32[]{:S(2)}) %collective-permute-start) | collective-permute-done | bytes 2097184 | tf_op jit(solution)/shard_map/ppermute | solution.py:225
  267.0 5.7 all-to-all-start.2
  274.7 8.4 %shard_map.38.rest_4_ = f32[2,16,256,1024]{3,2,1,0:T(8,128)} custom-call(s32[1]{0:T(128)} %bitcast.me_ref, bf16[8,2,2,32,1024]{4,3,2,1,0:T(8,128)(2,1)} %all_to_all.40.rest_0_, bf16[8,2,2,32,1024]{4,3,2,1,0:T(8,128)(2,1)} %copy-done.7, bf16[8,2,2,32,1024]{4,3,2,1,0:T(8,128)(2,1)} %copy-done.6, bf16[8,2,2,32,1024]{4,3,2,1,0:T(8,128)(2,1)} %collective-permute-done.2.rest_3_), custom_call_target="tpu_custom_call" | custom-call | flops 4294967296 | bytes 12582912 | tf_op jit(solution)/shard_map/pallas_call | solution.py:198
  283.2 33.6 %collective-permute-done.5.rest_2_ = bf16[8,2,2,32,1024]{4,3,2,1,0:T(8,128)(2,1)} collective-permute-done((bf16[8,2,2,32,1024]{4,3,2,1,0:T(8,128)(2,1)}, bf16[8,2,2,32,1024]{4,3,2,1,0:T(8,128)(2,1)}, u32[]{:S(2)}, u32[]{:S(2)}) %collective-permute-start.5) | collective-permute-done | bytes 2097184 | tf_op jit(solution)/shard_map/ppermute | solution.py:225
  319.2 4.7 all-to-all-start.5
  325.9 8.4 %shard_map.39.rest_4_ = f32[2,16,256,1024]{3,2,1,0:T(8,128)} custom-call(s32[1]{0:T(128)} %bitcast.me_ref, bf16[8,2,2,32,1024]{4,3,2,1,0:T(8,128)(2,1)} %copy-done.3, bf16[8,2,2,32,1024]{4,3,2,1,0:T(8,128)(2,1)} %collective-permute-done.9.rest_1_, bf16[8,2,2,32,1024]{4,3,2,1,0:T(8,128)(2,1)} %copy-done.5, ...), custom_call_target="tpu_custom_call", output_to_operand_aliasing={{}: (5, {})} | custom-call | flops 4294967296 | bytes 12582912 | tf_op jit(solution)/shard_map/pallas_call | solution.py:198
  334.3 35.9 %collective-permute-done.4.rest_2_ = bf16[8,2,2,32,1024]{4,3,2,1,0:T(8,128)(2,1)} collective-permute-done((bf16[8,2,2,32,1024]{4,3,2,1,0:T(8,128)(2,1)}, bf16[8,2,2,32,1024]{4,3,2,1,0:T(8,128)(2,1)}, u32[]{:S(2)}, u32[]{:S(2)}) %collective-permute-start.4) | collective-permute-done | bytes 2097184 | tf_op jit(solution)/shard_map/ppermute | solution.py:225
  371.1 4.9 all-to-all-start.4
  378.0 8.4 %shard_map.40.rest_4_ = f32[2,16,256,1024]{3,2,1,0:T(8,128)} custom-call(s32[1]{0:T(128)} %bitcast.me_ref, bf16[8,2,2,32,1024]{4,3,2,1,0:T(8,128)(2,1)} %copy-done.2, bf16[8,2,2,32,1024]{4,3,2,1,0:T(8,128)(2,1)} %collective-permute-done.7.rest_1_, bf16[8,2,2,32,1024]{4,3,2,1,0:T(8,128)(2,1)} %collective-permute-done.5.rest_2_, ...), custom_call_target="tpu_custom_call", output_to_operand_aliasing={{}: (5, {})} | custom-call | flops 4294967296 | bytes 12582912 | tf_op jit(solution)/shard_map/pallas_call | solution.py:198
  386.4 35.7 %collective-permute-done.11.rest_2_ = bf16[8,2,2,32,1024]{4,3,2,1,0:T(8,128)(2,1)} collective-permute-done((bf16[8,2,2,32,1024]{4,3,2,1,0:T(8,128)(2,1)S(1)}, bf16[8,2,2,32,1024]{4,3,2,1,0:T(8,128)(2,1)}, u32[]{:S(2)}, u32[]{:S(2)}) %collective-permute-start.11) | collective-permute-done | bytes 2097184 | tf_op jit(solution)/shard_map/ppermute | solution.py:225
  423.2 4.6 all-to-all-start.7
  429.9 8.4 %shard_map.41.rest_4_ = f32[2,16,256,1024]{3,2,1,0:T(8,128)} custom-call(s32[1]{0:T(128)} %bitcast.me_ref, bf16[8,2,2,32,1024]{4,3,2,1,0:T(8,128)(2,1)} %copy-done.1, bf16[8,2,2,32,1024]{4,3,2,1,0:T(8,128)(2,1)} %collective-permute-done.15.rest_1_, bf16[8,2,2,32,1024]{4,3,2,1,0:T(8,128)(2,1)} %collective-permute-done.4.rest_2_, ...), custom_call_target="tpu_custom_call", output_to_operand_aliasing={{}: (5, {})} | custom-call | flops 4294967296 | bytes 12582912 | tf_op jit(solution)/shard_map/pallas_call | solution.py:198
  438.3 36.1 %collective-permute-done.10.rest_2_ = bf16[8,2,2,32,1024]{4,3,2,1,0:T(8,128)(2,1)} collective-permute-done((bf16[8,2,2,32,1024]{4,3,2,1,0:T(8,128)(2,1)}, bf16[8,2,2,32,1024]{4,3,2,1,0:T(8,128)(2,1)}, u32[]{:S(2)}, u32[]{:S(2)}) %collective-permute-start.10) | collective-permute-done | bytes 2097184 | tf_op jit(solution)/shard_map/ppermute | solution.py:225
  475.4 4.8 all-to-all-start.6
  481.7 45.8 %all-to-all-done.6.rest_0_ = bf16[8,2,2,32,1024]{4,3,2,1,0:T(8,128)(2,1)S(1)} async-done(((bf16[8,2,2,32,1024]{4,3,2,1,0:T(8,128)(2,1)}), bf16[8,2,2,32,1024]{4,3,2,1,0:T(8,128)(2,1)S(1)}, u32[]{:S(2)}, u32[]{:S(2)}) %all-to-all-start.6) | async-done | bytes 2097184 | tf_op jit(solution)/shard_map/all_to_all | solution.py:248
  530.0 42.8 %collective-permute-done.17.rest_2_ = bf16[8,2,2,32,1024]{4,3,2,1,0:T(8,128)(2,1)} collective-permute-done((bf16[8,2,2,32,1024]{4,3,2,1,0:T(8,128)(2,1)S(1)}, bf16[8,2,2,32,1024]{4,3,2,1,0:T(8,128)(2,1)}, u32[]{:S(2)}, u32[]{:S(2)}) %collective-permute-start.17) | collective-permute-done | bytes 2097184 | tf_op jit(solution)/shard_map/ppermute | solution.py:225
  572.8 8.4 %shard_map.42.rest_4_ = f32[2,16,256,1024]{3,2,1,0:T(8,128)} custom-call(s32[1]{0:T(128)} %bitcast.me_ref, bf16[8,2,2,32,1024]{4,3,2,1,0:T(8,128)(2,1)} %copy-done, bf16[8,2,2,32,1024]{4,3,2,1,0:T(8,128)(2,1)} %collective-permute-done.13.rest_1_, bf16[8,2,2,32,1024]{4,3,2,1,0:T(8,128)(2,1)} %collective-permute-done.11.rest_2_, ...), custom_call_target="tpu_custom_call", output_to_operand_aliasing={{}: (5, {})} | custom-call | flops 4294967296 | bytes 12582912 | tf_op jit(solution)/shard_map/pallas_call | solution.py:198
  581.2 8.5 %shard_map.43.rest_4_ = f32[2,16,256,1024]{3,2,1,0:T(8,128)} custom-call(s32[1]{0:T(128)} %bitcast.me_ref, bf16[8,2,2,32,1024]{4,3,2,1,0:T(8,128)(2,1)} %all-to-all-done.4.rest_0_, bf16[8,2,2,32,1024]{4,3,2,1,0:T(8,128)(2,1)} %collective-permute-done.22.rest_1_, ...), custom_call_target="tpu_custom_call", output_to_operand_aliasing={{}: (5, {})} | custom-call | flops 4294967296 | bytes 12582912 | tf_op jit(solution)/shard_map/pallas_call | solution.py:198
  589.7 8.5 %shard_map.44.rest_4_ = f32[2,16,256,1024]{3,2,1,0:T(8,128)} custom-call(s32[1]{0:T(128)} %bitcast.me_ref, bf16[8,2,2,32,1024]{4,3,2,1,0:T(8,128)(2,1)} %all-to-all-done.7.rest_0_, bf16[8,2,2,32,1024]{4,3,2,1,0:T(8,128)(2,1)} %collective-permute-done.19.rest_1_, ...), custom_call_target="tpu_custom_call", output_to_operand_aliasing={{}: (5, {})} | custom-call | flops 4294967296 | bytes 12582912 | tf_op jit(solution)/shard_map/pallas_call | solution.py:198
  598.2 8.5 %shard_map.45 = f32[2,16,256,1024]{3,2,1,0:T(8,128)} custom-call(s32[1]{0:T(128)} %bitcast.me_ref, bf16[8,2,2,32,1024]{4,3,2,1,0:T(8,128)(2,1)} %copy-done.4, bf16[8,2,2,32,1024]{4,3,2,1,0:T(8,128)(2,1)} %collective-permute-done.16.rest_1_, bf16[8,2,2,32,1024]{4,3,2,1,0:T(8,128)(2,1)} %collective-permute-done.17.rest_2_, ...), custom_call_target="tpu_custom_call", output_to_operand_aliasing={{}: (5, {})} | custom-call | flops 4294967296 | bytes 12582912 | tf_op jit(solution)/shard_map/pallas_call | solution.py:198
  (73 shorter events, 38.8 us)
Async XLA Ops:
  158.6 51.9 %all-to-all-start = ((bf16[8,2,2,32,1024]{4,3,2,1,0:T(8,128)(2,1)}), bf16[8,2,2,32,1024]{4,3,2,1,0:T(8,128)(2,1)S(1)}, u32[]{:S(2)}, u32[]{:S(2)}) async-start(bf16[8,2,2,32,1024]{4,3,2,1,0:T(8,128)(2,1)} %get-tuple-element.51), calls=%async_computation | async-start | bytes 4194304 | tf_op jit(solution)/shard_map/all_to_all | solution.py:248
  162.2 46.9 %collective-permute-start.1 = (bf16[8,2,2,32,1024]{4,3,2,1,0:T(8,128)(2,1)}, bf16[8,2,2,32,1024]{4,3,2,1,0:T(8,128)(2,1)S(1)}, u32[]{:S(2)}, u32[]{:S(2)}) collective-permute-start(bf16[8,2,2,32,1024]{4,3,2,1,0:T(8,128)(2,1)} %all_to_all.40.rest_0_), channel_id=1, source_target_pairs={{0,2},{1,3},{2,0},{3,1},{4,6},{5,7},{6,4},{7,5},{8,10},{9,11},{10,... | collective-permute-start | bytes 6291464 | tf_op jit(solution)/shard_map/ppermute | solution.py:225
  211.8 53.9 %all-to-all-start.3 = ((bf16[8,2,2,32,1024]{4,3,2,1,0:T(8,128)(2,1)}), bf16[8,2,2,32,1024]{4,3,2,1,0:T(8,128)(2,1)S(1)}, u32[]{:S(2)}, u32[]{:S(2)}) async-start(bf16[8,2,2,32,1024]{4,3,2,1,0:T(8,128)(2,1)} %get-tuple-element.59), calls=%async_computation.3 | async-start | bytes 4194304 | tf_op jit(solution)/shard_map/all_to_all | solution.py:248
  217.6 45.5 %collective-permute-start = (bf16[8,2,2,32,1024]{4,3,2,1,0:T(8,128)(2,1)}, bf16[8,2,2,32,1024]{4,3,2,1,0:T(8,128)(2,1)S(1)}, u32[]{:S(2)}, u32[]{:S(2)}) collective-permute-start(bf16[8,2,2,32,1024]{4,3,2,1,0:T(8,128)(2,1)} %copy-done.3), channel_id=1, source_target_pairs={{0,2},{1,3},{2,0},{3,1},{4,6},{5,7},{6,4},{7,5},{8,10},{9,11},{10,... | collective-permute-start | bytes 6291464 | tf_op jit(solution)/shard_map/ppermute | solution.py:225
  219.1 46.7 %collective-permute-start.2 = (bf16[8,2,2,32,1024]{4,3,2,1,0:T(8,128)(2,1)}, bf16[8,2,2,32,1024]{4,3,2,1,0:T(8,128)(2,1)}, u32[]{:S(2)}, u32[]{:S(2)}) collective-permute-start(bf16[8,2,2,32,1024]{4,3,2,1,0:T(8,128)(2,1)} %copy-done.6), channel_id=1, source_target_pairs={{0,1},{1,0},{2,3},{3,2},{4,5},{5,4},{6,7},{7,6},{8,9},{9,8},{10,11... | collective-permute-start | bytes 6291464 | tf_op jit(solution)/shard_map/ppermute | solution.py:225
  267.0 50.9 %all-to-all-start.2 = ((bf16[8,2,2,32,1024]{4,3,2,1,0:T(8,128)(2,1)}), bf16[8,2,2,32,1024]{4,3,2,1,0:T(8,128)(2,1)S(1)}, u32[]{:S(2)}, u32[]{:S(2)}) async-start(bf16[8,2,2,32,1024]{4,3,2,1,0:T(8,128)(2,1)} %get-tuple-element.56), calls=%async_computation.2 | async-start | bytes 4194304 | tf_op jit(solution)/shard_map/all_to_all | solution.py:248
  319.2 51.8 %all-to-all-start.5 = ((bf16[8,2,2,32,1024]{4,3,2,1,0:T(8,128)(2,1)}), bf16[8,2,2,32,1024]{4,3,2,1,0:T(8,128)(2,1)S(1)}, u32[]{:S(2)}, u32[]{:S(2)}) async-start(bf16[8,2,2,32,1024]{4,3,2,1,0:T(8,128)(2,1)} %get-tuple-element.73), calls=%async_computation.5 | async-start | bytes 4194304 | tf_op jit(solution)/shard_map/all_to_all | solution.py:248
  323.9 46.3 %collective-permute-start.4 = (bf16[8,2,2,32,1024]{4,3,2,1,0:T(8,128)(2,1)}, bf16[8,2,2,32,1024]{4,3,2,1,0:T(8,128)(2,1)}, u32[]{:S(2)}, u32[]{:S(2)}) collective-permute-start(bf16[8,2,2,32,1024]{4,3,2,1,0:T(8,128)(2,1)} %copy-done.1), channel_id=1, source_target_pairs={{0,2},{1,3},{2,0},{3,1},{4,6},{5,7},{6,4},{7,5},{8,10},{9,11},{10,... | collective-permute-start | bytes 6291464 | tf_op jit(solution)/shard_map/ppermute | solution.py:225
  325.4 44.8 %collective-permute-start.7 = (bf16[8,2,2,32,1024]{4,3,2,1,0:T(8,128)(2,1)}, bf16[8,2,2,32,1024]{4,3,2,1,0:T(8,128)(2,1)}, u32[]{:S(2)}, u32[]{:S(2)}) collective-permute-start(bf16[8,2,2,32,1024]{4,3,2,1,0:T(8,128)(2,1)} %copy-done.2), channel_id=1, source_target_pairs={{0,1},{1,0},{2,3},{3,2},{4,5},{5,4},{6,7},{7,6},{8,9},{9,8},{10,11... | collective-permute-start | bytes 6291464 | tf_op jit(solution)/shard_map/ppermute | solution.py:225
  325.4 44.8 %collective-permute-start.6 = (bf16[8,2,2,32,1024]{4,3,2,1,0:T(8,128)(2,1)}, bf16[8,2,2,32,1024]{4,3,2,1,0:T(8,128)(2,1)}, u32[]{:S(2)}, u32[]{:S(2)}) collective-permute-start(bf16[8,2,2,32,1024]{4,3,2,1,0:T(8,128)(2,1)} %collective-permute-done.5.rest_2_), channel_id=1, source_target_pairs={{0,1},{1,0},{2,3},{3,2},{4,5},{5,4},{6,7},{7,6},{8,9},{9,8},{10,11... | collective-permute-start | bytes 6291464 | tf_op jit(solution)/shard_map/ppermute | solution.py:225
  371.1 52.2 %all-to-all-start.4 = ((bf16[8,2,2,32,1024]{4,3,2,1,0:T(8,128)(2,1)}), bf16[8,2,2,32,1024]{4,3,2,1,0:T(8,128)(2,1)}, u32[]{:S(2)}, u32[]{:S(2)}) async-start(bf16[8,2,2,32,1024]{4,3,2,1,0:T(8,128)(2,1)} %get-tuple-element.70), calls=%async_computation.4 | async-start | bytes 4194304 | tf_op jit(solution)/shard_map/all_to_all | solution.py:248
  376.0 46.1 %collective-permute-start.11 = (bf16[8,2,2,32,1024]{4,3,2,1,0:T(8,128)(2,1)S(1)}, bf16[8,2,2,32,1024]{4,3,2,1,0:T(8,128)(2,1)}, u32[]{:S(2)}, u32[]{:S(2)}) collective-permute-start(bf16[8,2,2,32,1024]{4,3,2,1,0:T(8,128)(2,1)S(1)} %all-to-all-done.5.rest_0_), channel_id=1, source_target_pairs={{0,2},{1,3},{2,0},{3,1},{4,6},{5,7},{6,4},{7,5},{8,10},{9,11},{10,... | collective-permute-start | bytes 6291464 | tf_op jit(solution)/shard_map/ppermute | solution.py:225
  423.2 52.2 %all-to-all-start.7 = ((bf16[8,2,2,32,1024]{4,3,2,1,0:T(8,128)(2,1)}), bf16[8,2,2,32,1024]{4,3,2,1,0:T(8,128)(2,1)}, u32[]{:S(2)}, u32[]{:S(2)}) async-start(bf16[8,2,2,32,1024]{4,3,2,1,0:T(8,128)(2,1)} %get-tuple-element.86), calls=%async_computation.7 | async-start | bytes 4194304 | tf_op jit(solution)/shard_map/all_to_all | solution.py:248
  427.8 46.6 %collective-permute-start.10 = (bf16[8,2,2,32,1024]{4,3,2,1,0:T(8,128)(2,1)}, bf16[8,2,2,32,1024]{4,3,2,1,0:T(8,128)(2,1)}, u32[]{:S(2)}, u32[]{:S(2)}) collective-permute-start(bf16[8,2,2,32,1024]{4,3,2,1,0:T(8,128)(2,1)} %all-to-all-done.4.rest_0_), channel_id=1, source_target_pairs={{0,2},{1,3},{2,0},{3,1},{4,6},{5,7},{6,4},{7,5},{8,10},{9,11},{10,... | collective-permute-start | bytes 6291464 | tf_op jit(solution)/shard_map/ppermute | solution.py:225
  429.4 45.1 %collective-permute-start.13 = (bf16[8,2,2,32,1024]{4,3,2,1,0:T(8,128)(2,1)S(1)}, bf16[8,2,2,32,1024]{4,3,2,1,0:T(8,128)(2,1)}, u32[]{:S(2)}, u32[]{:S(2)}) collective-permute-start(bf16[8,2,2,32,1024]{4,3,2,1,0:T(8,128)(2,1)S(1)} %all-to-all-done.5.rest_0_), channel_id=1, source_target_pairs={{0,1},{1,0},{2,3},{3,2},{4,5},{5,4},{6,7},{7,6},{8,9},{9,8},{10,11... | collective-permute-start | bytes 6291464 | tf_op jit(solution)/shard_map/ppermute | solution.py:225
  429.4 45.1 %collective-permute-start.12 = (bf16[8,2,2,32,1024]{4,3,2,1,0:T(8,128)(2,1)}, bf16[8,2,2,32,1024]{4,3,2,1,0:T(8,128)(2,1)}, u32[]{:S(2)}, u32[]{:S(2)}) collective-permute-start(bf16[8,2,2,32,1024]{4,3,2,1,0:T(8,128)(2,1)} %collective-permute-done.11.rest_2_), channel_id=1, source_target_pairs={{0,1},{1,0},{2,3},{3,2},{4,5},{5,4},{6,7},{7,6},{8,9},{9,8},{10,11... | collective-permute-start | bytes 6291464 | tf_op jit(solution)/shard_map/ppermute | solution.py:225
  475.4 52.1 %all-to-all-start.6 = ((bf16[8,2,2,32,1024]{4,3,2,1,0:T(8,128)(2,1)}), bf16[8,2,2,32,1024]{4,3,2,1,0:T(8,128)(2,1)S(1)}, u32[]{:S(2)}, u32[]{:S(2)}) async-start(bf16[8,2,2,32,1024]{4,3,2,1,0:T(8,128)(2,1)} %get-tuple-element.85), calls=%async_computation.6 | async-start | bytes 4194304 | tf_op jit(solution)/shard_map/all_to_all | solution.py:248
  480.2 49.3 %collective-permute-start.20 = (bf16[8,2,2,32,1024]{4,3,2,1,0:T(8,128)(2,1)}, bf16[8,2,2,32,1024]{4,3,2,1,0:T(8,128)(2,1)}, u32[]{:S(2)}, u32[]{:S(2)}) collective-permute-start(bf16[8,2,2,32,1024]{4,3,2,1,0:T(8,128)(2,1)} %all-to-all-done.7.rest_0_), channel_id=1, source_target_pairs={{0,2},{1,3},{2,0},{3,1},{4,6},{5,7},{6,4},{7,5},{8,10},{9,11},{10,... | collective-permute-start | bytes 6291464 | tf_op jit(solution)/shard_map/ppermute | solution.py:225
  481.7 47.8 %collective-permute-start.22 = (bf16[8,2,2,32,1024]{4,3,2,1,0:T(8,128)(2,1)}, bf16[8,2,2,32,1024]{4,3,2,1,0:T(8,128)(2,1)}, u32[]{:S(2)}, u32[]{:S(2)}) collective-permute-start(bf16[8,2,2,32,1024]{4,3,2,1,0:T(8,128)(2,1)} %all-to-all-done.4.rest_0_), channel_id=1, source_target_pairs={{0,1},{1,0},{2,3},{3,2},{4,5},{5,4},{6,7},{7,6},{8,9},{9,8},{10,11... | collective-permute-start | bytes 6291464 | tf_op jit(solution)/shard_map/ppermute | solution.py:225
  527.5 45.3 %collective-permute-start.17 = (bf16[8,2,2,32,1024]{4,3,2,1,0:T(8,128)(2,1)S(1)}, bf16[8,2,2,32,1024]{4,3,2,1,0:T(8,128)(2,1)}, u32[]{:S(2)}, u32[]{:S(2)}) collective-permute-start(bf16[8,2,2,32,1024]{4,3,2,1,0:T(8,128)(2,1)S(1)} %all-to-all-done.6.rest_0_), channel_id=1, source_target_pairs={{0,2},{1,3},{2,0},{3,1},{4,6},{5,7},{6,4},{7,5},{8,10},{9,11},{10,... | collective-permute-start | bytes 6291464 | tf_op jit(solution)/shard_map/ppermute | solution.py:225
  529.0 52.3 %collective-permute-start.23 = (bf16[8,2,2,32,1024]{4,3,2,1,0:T(8,128)(2,1)}, bf16[8,2,2,32,1024]{4,3,2,1,0:T(8,128)(2,1)}, u32[]{:S(2)}, u32[]{:S(2)}) collective-permute-start(bf16[8,2,2,32,1024]{4,3,2,1,0:T(8,128)(2,1)} %collective-permute-done.10.rest_2_), channel_id=1, source_target_pairs={{0,1},{1,0},{2,3},{3,2},{4,5},{5,4},{6,7},{7,6},{8,9},{9,8},{10,11... | collective-permute-start | bytes 6291464 | tf_op jit(solution)/shard_map/ppermute | solution.py:225
  529.0 60.8 %collective-permute-start.19 = (bf16[8,2,2,32,1024]{4,3,2,1,0:T(8,128)(2,1)}, bf16[8,2,2,32,1024]{4,3,2,1,0:T(8,128)(2,1)}, u32[]{:S(2)}, u32[]{:S(2)}) collective-permute-start(bf16[8,2,2,32,1024]{4,3,2,1,0:T(8,128)(2,1)} %all-to-all-done.7.rest_0_), channel_id=1, source_target_pairs={{0,1},{1,0},{2,3},{3,2},{4,5},{5,4},{6,7},{7,6},{8,9},{9,8},{10,11... | collective-permute-start | bytes 6291464 | tf_op jit(solution)/shard_map/ppermute | solution.py:225
  529.5 60.3 %collective-permute-start.21 = (bf16[8,2,2,32,1024]{4,3,2,1,0:T(8,128)(2,1)}, bf16[8,2,2,32,1024]{4,3,2,1,0:T(8,128)(2,1)}, u32[]{:S(2)}, u32[]{:S(2)}) collective-permute-start(bf16[8,2,2,32,1024]{4,3,2,1,0:T(8,128)(2,1)} %collective-permute-done.20.rest_2_), channel_id=1, source_target_pairs={{0,1},{1,0},{2,3},{3,2},{4,5},{5,4},{6,7},{7,6},{8,9},{9,8},{10,11... | collective-permute-start | bytes 6291464 | tf_op jit(solution)/shard_map/ppermute | solution.py:225
  529.5 68.7 %collective-permute-start.16 = (bf16[8,2,2,32,1024]{4,3,2,1,0:T(8,128)(2,1)S(1)}, bf16[8,2,2,32,1024]{4,3,2,1,0:T(8,128)(2,1)}, u32[]{:S(2)}, u32[]{:S(2)}) collective-permute-start(bf16[8,2,2,32,1024]{4,3,2,1,0:T(8,128)(2,1)S(1)} %all-to-all-done.6.rest_0_), channel_id=1, source_target_pairs={{0,1},{1,0},{2,3},{3,2},{4,5},{5,4},{6,7},{7,6},{8,9},{9,8},{10,11... | collective-permute-start | bytes 6291464 | tf_op jit(solution)/shard_map/ppermute | solution.py:225
  (15 other events, 408.1 us)

commit v2 on v1

v2 whole, which is shorter than its diff:
```python
import functools

import jax
import jax.numpy as jnp
from jax import lax
from jax.experimental import pallas as pl
from jax.experimental.pallas import tpu as pltpu
from jax.sharding import PartitionSpec as P

NFFT = 256
TAPS = 4
CH = 128
FRAMES = 1024
FIRST = 0
LANES = 128
VMEM = 60 * 1024 * 1024


def window_table(tap_count, length):
    count = tap_count * length
    sample_idx = jnp.arange(count).astype(jnp.float32)
    center = (count - 1) / 2.0
    shaped = jnp.sinc((sample_idx - center) / length) * (
        0.5 - 0.5 * jnp.cos(2.0 * jnp.pi * sample_idx / (count - 1))
    )
    return shaped.reshape(tap_count, length)


def fourier_table(length, channels, lowest, freq):
    owned = channels // freq
    row = jnp.arange(2 * channels, dtype=jnp.int32)
    place, part, dest = row // (2 * freq), row // freq % 2, row % freq
    channel_idx = dest * owned + place + lowest
    sample_idx = jnp.arange(length, dtype=jnp.int32)
    product = sample_idx[None, :] * channel_idx[:, None] % length
    angle = 2.0 * jnp.pi * product.astype(jnp.float32) / length
    factor = 1.0 / jnp.sqrt(jnp.float32(length))
    return jnp.where(part[:, None] == 0, jnp.cos(angle) * factor, -jnp.sin(angle) * factor).astype(
        jnp.bfloat16
    )


def chunk_sizes(channels):
    if channels == 16:
        return (2, 2, 2, 2, 2, 2, 2, 2)
    return (1,) * channels


def analyse_kernel(
    owned, freq, low, sizes, volt_ref, h0_ref, h1_ref, h2_ref, window_ref, table_ref, gre_ref, gim_ref, *rest
):
    outs, (low_ref, high_ref, spec_ref, wre_ref, wim_ref) = rest[: len(sizes)], rest[len(sizes) :]
    halos = (h0_ref, h1_ref, h2_ref)

    @pl.when(pl.program_id(0) == 0)
    def _():
        for source, spread in ((gre_ref, wre_ref), (gim_ref, wim_ref)):
            gain = source[...]
            for c in range(CH):
                spread[c * owned : (c + 1) * owned, :] = jnp.broadcast_to(
                    gain[:, c : c + 1], (owned, LANES)
                )

    group = 8
    last = LANES // group - 1
    for half, ref in enumerate((low_ref, high_ref)):
        lanes = slice(half * LANES, (half + 1) * LANES)
        weights = [
            jnp.broadcast_to(window_ref[p : p + 1, lanes], (owned, LANES)) for p in range(TAPS)
        ]

        def load(position, half=half):
            at = pl.ds(pl.multiple_of(position * NFFT + half * LANES, LANES), LANES)
            return volt_ref[:, at].astype(jnp.float32)

        def emit(position, taps, weights=weights, ref=ref):
            total = weights[0] * taps[0]
            for p in range(1, TAPS):
                total = total + weights[p] * taps[p]
            ref[pl.ds(pl.multiple_of(position * owned, owned), owned), :] = total

        def step(g, carry, load=load, emit=emit):
            taps = list(carry)
            for u in range(group):
                taps.append(load(g * group + u + TAPS - 1))
                emit(g * group + u, taps[-TAPS:])
            return tuple(taps[1 - TAPS :])

        taps = list(lax.fori_loop(0, last, step, tuple(load(p) for p in range(TAPS - 1))))
        for position in range(last * group, LANES):
            ahead = position + TAPS - 1
            if ahead < LANES:
                taps.append(load(ahead))
            else:
                taps.append(halos[ahead - LANES][:, lanes].astype(jnp.float32))
            emit(position, taps[-TAPS:])

    pair = 2
    rows_of = lambda place: 2 * freq * place
    count = rows_of(sum(sizes))
    table = table_ref[rows_of(low) : rows_of(low) + count, :]
    for g in range(owned // pair):
        rows = jnp.concatenate(
            [
                jnp.concatenate(
                    [ref[pl.ds(g * pair + u, LANES, stride=owned), :] for ref in (low_ref, high_ref)],
                    axis=1,
                )
                for u in range(pair)
            ],
            axis=0,
        ).astype(jnp.bfloat16)
        result = lax.dot_general(
            table, rows, (((1,), (1,)), ((), ())), preferred_element_type=jnp.float32
        )
        for u in range(pair):
            spec_ref[pl.ds(g * pair + u, count, stride=owned), :] = result[
                :, u * LANES : (u + 1) * LANES
            ]

    channels = CH // freq
    start = 0
    for k, size in enumerate(sizes):
        for u in range(size):
            for dest in range(freq):
                row = (rows_of(start + u) + dest) * owned
                re = spec_ref[row : row + owned, :]
                im = spec_ref[row + freq * owned : row + (freq + 1) * owned, :]
                at = (dest * channels + low + start + u) * owned
                wre, wim = wre_ref[at : at + owned, :], wim_ref[at : at + owned, :]
                outs[k][dest, u, 0] = (wre * re - wim * im).astype(jnp.bfloat16)
                outs[k][dest, u, 1] = (wre * im + wim * re).astype(jnp.bfloat16)
        start += size


def analyse(voltages, window, table, gain_re, gain_im, freq, low, sizes, first, count):
    owned = voltages.shape[0]
    halo = [
        pl.BlockSpec((owned, NFFT), lambda b, q=q: (0, (first + b + 1) * LANES + q))
        for q in range(TAPS - 1)
    ]
    whole = lambda shape: pl.BlockSpec(shape, lambda b: (0, 0))
    return pl.pallas_call(
        functools.partial(analyse_kernel, owned, freq, low, sizes),
        grid=(count,),
        in_specs=[
            pl.BlockSpec((owned, LANES * NFFT), lambda b: (0, first + b)),
            *halo,
            whole((TAPS, NFFT)),
            whole((2 * CH, NFFT)),
            whole((owned, CH)),
            whole((owned, CH)),
        ],
        out_specs=[
            pl.BlockSpec((freq, size, 2, owned, LANES), lambda b: (0, 0, 0, 0, b)) for size in sizes
        ],
        out_shape=[
            jax.ShapeDtypeStruct((freq, size, 2, owned, count * LANES), jnp.bfloat16)
            for size in sizes
        ],
        scratch_shapes=[
            pltpu.VMEM((LANES * owned, LANES), jnp.float32),
            pltpu.VMEM((LANES * owned, LANES), jnp.float32),
            pltpu.VMEM((2 * freq * sum(sizes) * owned, LANES), jnp.float32),
            pltpu.VMEM((CH * owned, LANES), jnp.float32),
            pltpu.VMEM((CH * owned, LANES), jnp.float32),
        ],
        compiler_params=pltpu.CompilerParams(vmem_limit_bytes=VMEM),
        cost_estimate=pl.CostEstimate(
            flops=2 * owned * count * LANES * NFFT * 2 * CH * 8,
            bytes_accessed=4 * owned * count * LANES * NFFT,
            transcendentals=0,
        ),
    )(voltages, voltages, voltages, voltages, window, table, gain_re, gain_im)


def correlate_kernel(tiles, me_ref, *rest):
    heads, bodies, out_ref, left_ref = rest[:tiles], rest[tiles : 2 * tiles], rest[-2], rest[-1]
    rows = heads[0].shape[0] * heads[0].shape[3]

    def part(r, p):
        return [ref[r][:, 0, p].reshape(rows, -1) for ref in (heads, bodies)]

    re = jnp.concatenate(part(0, 0), axis=1)
    im = jnp.concatenate(part(0, 1), axis=1)
    left_ref[0:rows, 0:FRAMES] = re
    left_ref[0:rows, FRAMES:] = im
    left_ref[rows:, 0:FRAMES] = im
    left_ref[rows:, FRAMES:] = -re
    factor = 1.0 / FRAMES
    for r in range(tiles):
        other = jnp.concatenate([*part(r, 0), *part(r, 1)], axis=1)
        both = lax.dot_general(
            left_ref[...], other, (((1,), (1,)), ((), ())), preferred_element_type=jnp.float32
        )
        at = pl.ds(pl.multiple_of((me_ref[0] ^ r) * rows, rows), rows)
        out_ref[0, 0, :, at] = both[:rows] * factor
        out_ref[1, 0, :, at] = both[rows:] * factor


def correlate(me, heads, bodies, previous, first, channels):
    freq, size, _, owned, _ = bodies[0].shape
    tiles = len(bodies)
    rows = freq * owned
    in_specs = [
        pl.BlockSpec((freq, 1, 2, owned, x.shape[-1]), lambda c, me: (0, first + c, 0, 0, 0))
        for x in heads
    ] + [
        pl.BlockSpec((freq, 1, 2, owned, x.shape[-1]), lambda c, me: (0, c, 0, 0, 0)) for x in bodies
    ]
    args = [me, *heads, *bodies]
    aliases = {}
    if previous is not None:
        in_specs.append(pl.BlockSpec(memory_space=pl.ANY))
        aliases = {len(args): 0}
        args.append(previous)
    return pl.pallas_call(
        functools.partial(correlate_kernel, tiles),
        grid_spec=pltpu.PrefetchScalarGridSpec(
            num_scalar_prefetch=1,
            grid=(size,),
            in_specs=in_specs,
            out_specs=pl.BlockSpec((2, 1, rows, tiles * rows), lambda c, me: (0, first + c, 0, 0)),
            scratch_shapes=[pltpu.VMEM((2 * rows, 2 * FRAMES), jnp.bfloat16)],
        ),
        out_shape=jax.ShapeDtypeStruct((2, channels, rows, tiles * rows), jnp.float32),
        input_output_aliases=aliases,
        compiler_params=pltpu.CompilerParams(vmem_limit_bytes=VMEM),
        cost_estimate=pl.CostEstimate(
            flops=size * 2 * (2 * rows) * (2 * FRAMES) * (tiles * rows),
            bytes_accessed=size * (tiles * rows * FRAMES * 4 + 2 * rows * tiles * rows * 4),
            transcendentals=0,
        ),
    )(*args)


def per_device(freq, tile, voltages, gain_re, gain_im):
    channels = CH // freq
    sizes = chunk_sizes(channels)
    me = lax.axis_index("tile").astype(jnp.int32).reshape(1)
    tables = (
        window_table(TAPS, NFFT),
        fourier_table(NFFT, CH, FIRST, freq),
        gain_re,
        gain_im,
    )
    blocks = FRAMES // LANES
    messages = list(analyse(voltages, *tables, freq, 0, (channels,), 0, 1))
    lead = len(sizes) // 4
    messages += analyse(voltages, *tables, freq, 0, sizes[:lead], 1, blocks - 1)
    messages[1], again = lax.optimization_barrier((messages[1], voltages))
    messages += analyse(again, *tables, freq, sum(sizes[:lead]), sizes[lead:], 1, blocks - 1)

    def swap(array, bit):
        return lax.ppermute(array, "tile", [(t, t ^ bit) for t in range(tile)])

    count = len(messages)
    firsts = [sum(sizes[:k]) for k in range(count)]
    turned, across, beside, opposite, results = ([None] * count for _ in range(5))

    def finish(k):
        heads, bodies = (
            [turned[m], beside[m], across[m], opposite[m]] for m in (0, k)
        )
        results[k] = correlate(me, heads, bodies, results[k - 1], firsts[k - 1], channels)

    def after(array, *waits):
        waits = [w for w in waits if w is not None]
        return lax.optimization_barrier((array, *waits))[0] if waits else array

    lag = 2
    for k in range(count):
        message = messages[k]
        if k >= lag:
            message = after(message, across[k - lag], beside[k - lag])
        if k >= lag + 1:
            message = after(message, opposite[k - lag - 1])
        if k >= lag + 2:
            message = after(message, results[k - lag - 2])
        turned[k] = lax.all_to_all(message, "freq", split_axis=0, concat_axis=0, tiled=True)
        across[k] = swap(turned[k], 2)
        beside[k] = swap(turned[k], 1)
        source = across[k]
        if k == count - 1:
            source = after(source, results[k - 1])
        opposite[k] = swap(source, 1)
        if k >= 1:
            finish(k)
    return results[-1]


def solution(mesh):
    in_specs = (P(("tile", "freq"), None), P(("tile", "freq"), None), P(("tile", "freq"), None))
    out_specs = P(None, "freq", "tile", None)
    return jax.shard_map(
        functools.partial(per_device, mesh.shape["freq"], mesh.shape["tile"]),
        mesh=mesh,
        in_specs=in_specs,
        out_specs=out_specs,
        check_vma=False,
    )
```

time: 608 us -> 519 us (0.85)
  blocking collectives: 55.6 us -> 0 us
  waiting for transfers between devices: 323 us -> 287 us
  starting transfers between devices: 49.6 us -> 58.7 us
    all_to_all x1 -> x0, blocking collectives: 55.6 us -> none  [per_device(): lax.all_to_all(message, 'freq', split_axis=0, concat_axis=0, tiled=True)]
    all_to_all x7 -> x9, waiting for transfers between devices: 49.7 us -> 18.3 us  [per_device(): lax.all_to_all(message, 'freq', split_axis=0, concat_axis=0, tiled=True)]
    all_to_all x7 -> x9, starting transfers between devices: 34 us -> 48.3 us  [per_device(): lax.all_to_all(message, 'freq', split_axis=0, concat_axis=0, tiled=True)]
    ppermute x24 -> x27, starting transfers between devices: 15.6 us -> 10.4 us  [swap(): return lax.ppermute(array, 'tile', [(t, t ^ bit) for t in range(tile)])]
    ppermute x24 -> x27, waiting for transfers between devices: 273 us -> 269 us  [swap(): return lax.ppermute(array, 'tile', [(t, t ^ bit) for t in range(tile)])]
    pallas_call x1 -> x3, Pallas kernels: 95.4 us -> 93.2 us  [analyse(): pl.pallas_call(functools.partial(analyse_kernel, owned, freq, low, sizes)...]
  transfers between devices with their start and end apart: 31 -> 36, of which waited for: 12 -> 15; matrix products, arithmetic and copies ran while one was open for 0% -> 0% of each run, Pallas kernels for 10% -> 27%
where the time goes in v2:
time: 519 us; the launch traced here: 518 us
  waiting for transfers between devices  287 us (55%)
  Pallas kernels  162 us (31%)
  starting transfers between devices  58.7 us (11%)
  local copies, waits for them, and re-layouts  8.28 us (2%)
    ppermute x27, waiting for transfers between devices, swap(): return lax.ppermute(array, 'tile', [(t, t ^ bit) for t in range(tile)])  269 us
    pallas_call x3, Pallas kernels, analyse(): pl.pallas_call(functools.partial(analyse_kernel, owned, freq, low, sizes)...  93.2 us
    pallas_call x8, Pallas kernels, correlate(): pl.pallas_call(functools.partial(correlate_kernel, tiles), grid_spec=pltp...  68.4 us
    all_to_all x9, starting transfers between devices, per_device(): lax.all_to_all(message, 'freq', split_axis=0, concat_axis=0, tiled=True)  48.3 us
    all_to_all x9, waiting for transfers between devices, per_device(): lax.all_to_all(message, 'freq', split_axis=0, concat_axis=0, tiled=True)  18.3 us
    ppermute x27, starting transfers between devices, swap(): return lax.ppermute(array, 'tile', [(t, t ^ bit) for t in range(tile)])  10.4 us
  transfers between devices with their start and end apart: 36, of which 15 were waited for; matrix products, arithmetic and copies ran while one was open for 0% of the time, Pallas kernels for 27%

profile of v2, /device:TPU:0, one launch (start us, length us, event | category | flops | bytes accessed | tf_op | source)
XLA Modules:
  0.0 518.4 jit_solution(11242318704622303128)
XLA Ops:
  2.6 11.6 %shard_map.37 = bf16[8,16,2,32,128]{4,3,2,1,0:T(8,128)(2,1)} custom-call(bf16[32,262912]{1,0:T(8,128)(2,1)} %h2_ref.4, bf16[32,262912]{1,0:T(8,128)(2,1)} %h2_ref.4, bf16[32,262912]{1,0:T(8,128)(2,1)} %h2_ref.4, bf16[32,262912]{1,0:T(8,128)(2,1)} %h2_ref.4, f32[4,256]{1,0:T(4,128)} %fusion.11.window_ref, bf16[256,256]{1,0:T(8,128)(2,1)} %select_convert_fusion.table_ref, ...), custom_call_target="tpu_custom_call" | custom-call | flops 4294967296 | bytes 4194304 | tf_op jit(solution)/shard_map/pallas_call | solution.py:143
  14.1 7.3 %all-to-all-start = ((bf16[8,16,2,32,128]{4,3,2,1,0:T(8,128)(2,1)}), bf16[8,16,2,32,128]{4,3,2,1,0:T(8,128)(2,1)S(1)}, u32[]{:S(2)}, u32[]{:S(2)}) async-start(bf16[8,16,2,32,128]{4,3,2,1,0:T(8,128)(2,1)} %shard_map.37), calls=%async_computation | async-start | bytes 4194304 | tf_op jit(solution)/shard_map/all_to_all | solution.py:280
  21.4 34.9 %shard_map.38 = (bf16[8,2,2,32,896]{4,3,2,1,0:T(8,128)(2,1)}, bf16[8,2,2,32,896]{4,3,2,1,0:T(8,128)(2,1)}) custom-call(bf16[32,262912]{1,0:T(8,128)(2,1)} %h2_ref.4, bf16[32,262912]{1,0:T(8,128)(2,1)} %h2_ref.4, bf16[32,262912]{1,0:T(8,128)(2,1)} %h2_ref.4, bf16[32,262912]{1,0:T(8,128)(2,1)} %h2_ref.4, f32[4,256]{1,0:T(4,128)} %fusion.11.window_ref, ...), custom_call_target="tpu_custom_call" | custom-call | flops 30064771072 | bytes 29360128 | tf_op jit(solution)/shard_map/pallas_call | solution.py:143
  56.3 13.3 %all-to-all-done.rest_0_ = bf16[8,16,2,32,128]{4,3,2,1,0:T(8,128)(2,1)S(1)} async-done(((bf16[8,16,2,32,128]{4,3,2,1,0:T(8,128)(2,1)}), bf16[8,16,2,32,128]{4,3,2,1,0:T(8,128)(2,1)S(1)}, u32[]{:S(2)}, u32[]{:S(2)}) %all-to-all-start) | async-done | bytes 2097184 | tf_op jit(solution)/shard_map/all_to_all | solution.py:280
  75.5 45.0 %collective-permute-done.1.rest_2_ = bf16[8,16,2,32,128]{4,3,2,1,0:T(8,128)(2,1)S(1)} collective-permute-done((bf16[8,16,2,32,128]{4,3,2,1,0:T(8,128)(2,1)S(1)}, bf16[8,16,2,32,128]{4,3,2,1,0:T(8,128)(2,1)S(1)}, u32[]{:S(2)}, u32[]{:S(2)}) %collective-permute-start.1) | collective-permute-done | bytes 2097184 | tf_op jit(solution)/shard_map/ppermute | solution.py:255
  123.3 5.8 %all-to-all-start.1 = ((bf16[8,2,2,32,896]{4,3,2,1,0:T(8,128)(2,1)}), bf16[8,2,2,32,896]{4,3,2,1,0:T(8,128)(2,1)}, u32[]{:S(2)}, u32[]{:S(2)}) async-start(bf16[8,2,2,32,896]{4,3,2,1,0:T(8,128)(2,1)} %get-tuple-element.39), calls=%async_computation.1 | async-start | bytes 3670016 | tf_op jit(solution)/shard_map/all_to_all | solution.py:280
  131.2 46.7 %shard_map.39 = (bf16[8,2,2,32,896]{4,3,2,1,0:T(8,128)(2,1)}, bf16[8,2,2,32,896]{4,3,2,1,0:T(8,128)(2,1)}, bf16[8,2,2,32,896]{4,3,2,1,0:T(8,128)(2,1)}, bf16[8,2...) custom-call(bf16[32,262912]{1,0:T(8,128)(2,1)} %h2_ref.4, ...), custom_call_target="tpu_custom_call" | custom-call | flops 30064771072 | bytes 29360128 | tf_op jit(solution)/shard_map/pallas_call | solution.py:143
  177.9 6.0 %all-to-all-start.4 = ((bf16[8,2,2,32,896]{4,3,2,1,0:T(8,128)(2,1)}), bf16[8,2,2,32,896]{4,3,2,1,0:T(8,128)(2,1)S(1)}, u32[]{:S(2)}, u32[]{:S(2)}) async-start(bf16[8,2,2,32,896]{4,3,2,1,0:T(8,128)(2,1)} %get-tuple-element.46), calls=%async_computation.4 | async-start | bytes 3670016 | tf_op jit(solution)/shard_map/all_to_all | solution.py:280
  185.0 40.8 %collective-permute-done.3.rest_6_ = bf16[8,2,2,32,896]{4,3,2,1,0:T(8,128)(2,1)S(1)} collective-permute-done((bf16[8,2,2,32,896]{4,3,2,1,0:T(8,128)(2,1)}, bf16[8,2,2,32,896]{4,3,2,1,0:T(8,128)(2,1)S(1)}, u32[]{:S(2)}, u32[]{:S(2)}) %collective-permute-start.3) | collective-permute-done | bytes 1835040 | tf_op jit(solution)/shard_map/ppermute | solution.py:255
  228.9 5.7 %all-to-all-start.3 = ((bf16[8,2,2,32,896]{4,3,2,1,0:T(8,128)(2,1)}), bf16[8,2,2,32,896]{4,3,2,1,0:T(8,128)(2,1)S(1)}, u32[]{:S(2)}, u32[]{:S(2)}) async-start(bf16[8,2,2,32,896]{4,3,2,1,0:T(8,128)(2,1)} %get-tuple-element.42), calls=%async_computation.3 | async-start | bytes 3670016 | tf_op jit(solution)/shard_map/all_to_all | solution.py:280
  235.6 8.5 %shard_map.40.rest_8_ = f32[2,16,256,1024]{3,2,1,0:T(8,128)} custom-call(s32[1]{0:T(128)} %bitcast.me_ref, bf16[8,16,2,32,128]{4,3,2,1,0:T(8,128)(2,1)} %copy-done, bf16[8,16,2,32,128]{4,3,2,1,0:T(8,128)(2,1)} %copy-done.3, bf16[8,16,2,32,128]{4,3,2,1,0:T(8,128)(2,1)} %copy-done.1, bf16[8,16,2,32,128]{4,3,2,1,0:T(8,128)(2,1)} %collective-permute-done.2.rest_3_, ...), custom_call_target="tpu_custom_call" | custom-call | flops 4294967296 | bytes 12582912 | tf_op jit(solution)/shard_map/pallas_call | solution.py:217
  244.2 30.9 %collective-permute-done.10.rest_6_ = bf16[8,2,2,32,896]{4,3,2,1,0:T(8,128)(2,1)} collective-permute-done((bf16[8,2,2,32,896]{4,3,2,1,0:T(8,128)(2,1)}, bf16[8,2,2,32,896]{4,3,2,1,0:T(8,128)(2,1)}, u32[]{:S(2)}, u32[]{:S(2)}) %collective-permute-start.10) | collective-permute-done | bytes 1835040 | tf_op jit(solution)/shard_map/ppermute | solution.py:255
  283.1 8.5 %shard_map.41.rest_8_ = f32[2,16,256,1024]{3,2,1,0:T(8,128)} custom-call(s32[1]{0:T(128)} %bitcast.me_ref, bf16[8,16,2,32,128]{4,3,2,1,0:T(8,128)(2,1)} %copy-done, bf16[8,16,2,32,128]{4,3,2,1,0:T(8,128)(2,1)} %copy-done.3, bf16[8,16,2,32,128]{4,3,2,1,0:T(8,128)(2,1)} %copy-done.1, ...), custom_call_target="tpu_custom_call", output_to_operand_aliasing={{}: (9, {})} | custom-call | flops 4294967296 | bytes 12582912 | tf_op jit(solution)/shard_map/pallas_call | solution.py:217
  291.6 31.1 %collective-permute-done.7.rest_6_ = bf16[8,2,2,32,896]{4,3,2,1,0:T(8,128)(2,1)} collective-permute-done((bf16[8,2,2,32,896]{4,3,2,1,0:T(8,128)(2,1)}, bf16[8,2,2,32,896]{4,3,2,1,0:T(8,128)(2,1)}, u32[]{:S(2)}, u32[]{:S(2)}) %collective-permute-start.7) | collective-permute-done | bytes 1835040 | tf_op jit(solution)/shard_map/ppermute | solution.py:255
  329.5 8.5 %shard_map.42.rest_8_ = f32[2,16,256,1024]{3,2,1,0:T(8,128)} custom-call(s32[1]{0:T(128)} %bitcast.me_ref, bf16[8,16,2,32,128]{4,3,2,1,0:T(8,128)(2,1)} %copy-done, bf16[8,16,2,32,128]{4,3,2,1,0:T(8,128)(2,1)} %copy-done.3, bf16[8,16,2,32,128]{4,3,2,1,0:T(8,128)(2,1)} %copy-done.1, ...), custom_call_target="tpu_custom_call", output_to_operand_aliasing={{}: (9, {})} | custom-call | flops 4294967296 | bytes 12582912 | tf_op jit(solution)/shard_map/pallas_call | solution.py:217
  338.1 30.8 %collective-permute-done.16.rest_6_ = bf16[8,2,2,32,896]{4,3,2,1,0:T(8,128)(2,1)} collective-permute-done((bf16[8,2,2,32,896]{4,3,2,1,0:T(8,128)(2,1)S(1)}, bf16[8,2,2,32,896]{4,3,2,1,0:T(8,128)(2,1)}, u32[]{:S(2)}, u32[]{:S(2)}) %collective-permute-start.16) | collective-permute-done | bytes 1835040 | tf_op jit(solution)/shard_map/ppermute | solution.py:255
  375.7 8.5 %shard_map.43.rest_8_ = f32[2,16,256,1024]{3,2,1,0:T(8,128)} custom-call(s32[1]{0:T(128)} %bitcast.me_ref, bf16[8,16,2,32,128]{4,3,2,1,0:T(8,128)(2,1)} %copy-done, bf16[8,16,2,32,128]{4,3,2,1,0:T(8,128)(2,1)} %copy-done.3, bf16[8,16,2,32,128]{4,3,2,1,0:T(8,128)(2,1)} %copy-done.1, ...), custom_call_target="tpu_custom_call", output_to_operand_aliasing={{}: (9, {})} | custom-call | flops 4294967296 | bytes 12582912 | tf_op jit(solution)/shard_map/pallas_call | solution.py:217
  384.2 31.4 %collective-permute-done.13.rest_6_ = bf16[8,2,2,32,896]{4,3,2,1,0:T(8,128)(2,1)} collective-permute-done((bf16[8,2,2,32,896]{4,3,2,1,0:T(8,128)(2,1)}, bf16[8,2,2,32,896]{4,3,2,1,0:T(8,128)(2,1)}, u32[]{:S(2)}, u32[]{:S(2)}) %collective-permute-start.13) | collective-permute-done | bytes 1835040 | tf_op jit(solution)/shard_map/ppermute | solution.py:255
  422.4 39.4 %collective-permute-done.23.rest_6_ = bf16[8,2,2,32,896]{4,3,2,1,0:T(8,128)(2,1)} collective-permute-done((bf16[8,2,2,32,896]{4,3,2,1,0:T(8,128)(2,1)S(1)}, bf16[8,2,2,32,896]{4,3,2,1,0:T(8,128)(2,1)}, u32[]{:S(2)}, u32[]{:S(2)}) %collective-permute-start.23) | collective-permute-done | bytes 1835040 | tf_op jit(solution)/shard_map/ppermute | solution.py:255
  463.5 8.5 %shard_map.44.rest_8_ = f32[2,16,256,1024]{3,2,1,0:T(8,128)} custom-call(s32[1]{0:T(128)} %bitcast.me_ref, bf16[8,16,2,32,128]{4,3,2,1,0:T(8,128)(2,1)} %copy-done, bf16[8,16,2,32,128]{4,3,2,1,0:T(8,128)(2,1)} %copy-done.3, bf16[8,16,2,32,128]{4,3,2,1,0:T(8,128)(2,1)} %copy-done.1, ...), custom_call_target="tpu_custom_call", output_to_operand_aliasing={{}: (9, {})} | custom-call | flops 4294967296 | bytes 12582912 | tf_op jit(solution)/shard_map/pallas_call | solution.py:217
  472.1 8.6 %shard_map.45.rest_8_ = f32[2,16,256,1024]{3,2,1,0:T(8,128)} custom-call(s32[1]{0:T(128)} %bitcast.me_ref, bf16[8,16,2,32,128]{4,3,2,1,0:T(8,128)(2,1)} %copy-done, bf16[8,16,2,32,128]{4,3,2,1,0:T(8,128)(2,1)} %copy-done.3, bf16[8,16,2,32,128]{4,3,2,1,0:T(8,128)(2,1)} %copy-done.1, ...), custom_call_target="tpu_custom_call", output_to_operand_aliasing={{}: (9, {})} | custom-call | flops 4294967296 | bytes 12582912 | tf_op jit(solution)/shard_map/pallas_call | solution.py:217
  480.7 8.6 %shard_map.46.rest_8_ = f32[2,16,256,1024]{3,2,1,0:T(8,128)} custom-call(s32[1]{0:T(128)} %bitcast.me_ref, bf16[8,16,2,32,128]{4,3,2,1,0:T(8,128)(2,1)} %copy-done, bf16[8,16,2,32,128]{4,3,2,1,0:T(8,128)(2,1)} %copy-done.3, bf16[8,16,2,32,128]{4,3,2,1,0:T(8,128)(2,1)} %copy-done.1, ...), custom_call_target="tpu_custom_call", output_to_operand_aliasing={{}: (9, {})} | custom-call | flops 4294967296 | bytes 12582912 | tf_op jit(solution)/shard_map/pallas_call | solution.py:217
  489.3 15.3 %collective-permute-done.20.rest_6_ = bf16[8,2,2,32,896]{4,3,2,1,0:T(8,128)(2,1)} collective-permute-done((bf16[8,2,2,32,896]{4,3,2,1,0:T(8,128)(2,1)}, bf16[8,2,2,32,896]{4,3,2,1,0:T(8,128)(2,1)}, u32[]{:S(2)}, u32[]{:S(2)}) %collective-permute-start.20) | collective-permute-done | bytes 1835040 | tf_op jit(solution)/shard_map/ppermute | solution.py:255
  509.8 8.5 %shard_map.47 = f32[2,16,256,1024]{3,2,1,0:T(8,128)} custom-call(s32[1]{0:T(128)} %bitcast.me_ref, bf16[8,16,2,32,128]{4,3,2,1,0:T(8,128)(2,1)} %copy-done, bf16[8,16,2,32,128]{4,3,2,1,0:T(8,128)(2,1)} %copy-done.3, bf16[8,16,2,32,128]{4,3,2,1,0:T(8,128)(2,1)} %copy-done.1, ...), custom_call_target="tpu_custom_call", output_to_operand_aliasing={{}: (9, {})} | custom-call | flops 4294967296 | bytes 12582912 | tf_op jit(solution)/shard_map/pallas_call | solution.py:217
  (85 shorter events, 53.7 us)
Async XLA Ops:
  14.1 55.5 %all-to-all-start = ((bf16[8,16,2,32,128]{4,3,2,1,0:T(8,128)(2,1)}), bf16[8,16,2,32,128]{4,3,2,1,0:T(8,128)(2,1)S(1)}, u32[]{:S(2)}, u32[]{:S(2)}) async-start(bf16[8,16,2,32,128]{4,3,2,1,0:T(8,128)(2,1)} %shard_map.37), calls=%async_computation | async-start | bytes 4194304 | tf_op jit(solution)/shard_map/all_to_all | solution.py:280
  69.7 53.6 %all-to-all-start.2 = ((bf16[8,2,2,32,896]{4,3,2,1,0:T(8,128)(2,1)}), bf16[8,2,2,32,896]{4,3,2,1,0:T(8,128)(2,1)}, u32[]{:S(2)}, u32[]{:S(2)}) async-start(bf16[8,2,2,32,896]{4,3,2,1,0:T(8,128)(2,1)} %get-tuple-element.41), calls=%async_computation.2 | async-start | bytes 3670016 | tf_op jit(solution)/shard_map/all_to_all | solution.py:280
  74.0 46.6 %collective-permute-start.1 = (bf16[8,16,2,32,128]{4,3,2,1,0:T(8,128)(2,1)S(1)}, bf16[8,16,2,32,128]{4,3,2,1,0:T(8,128)(2,1)S(1)}, u32[]{:S(2)}, u32[]{:S(2)}) collective-permute-start(bf16[8,16,2,32,128]{4,3,2,1,0:T(8,128)(2,1)S(1)} %all-to-all-done.rest_0_), channel_id=1, source_target_pairs={{0,2},{1,3},{2,0},{3,1},{4,6},{5,7},{6,4},{7,5},{8,10},{9,11},{10,... | collective-permute-start | bytes 6291464 | tf_op jit(solution)/shard_map/ppermute | solution.py:255
  75.5 45.0 %collective-permute-start = (bf16[8,16,2,32,128]{4,3,2,1,0:T(8,128)(2,1)S(1)}, bf16[8,16,2,32,128]{4,3,2,1,0:T(8,128)(2,1)S(1)}, u32[]{:S(2)}, u32[]{:S(2)}) collective-permute-start(bf16[8,16,2,32,128]{4,3,2,1,0:T(8,128)(2,1)S(1)} %all-to-all-done.rest_0_), channel_id=1, source_target_pairs={{0,1},{1,0},{2,3},{3,2},{4,5},{5,4},{6,7},{7,6},{8,9},{9,8},{10,11... | collective-permute-start | bytes 6291464 | tf_op jit(solution)/shard_map/ppermute | solution.py:255
  123.3 54.6 %all-to-all-start.1 = ((bf16[8,2,2,32,896]{4,3,2,1,0:T(8,128)(2,1)}), bf16[8,2,2,32,896]{4,3,2,1,0:T(8,128)(2,1)}, u32[]{:S(2)}, u32[]{:S(2)}) async-start(bf16[8,2,2,32,896]{4,3,2,1,0:T(8,128)(2,1)} %get-tuple-element.39), calls=%async_computation.1 | async-start | bytes 3670016 | tf_op jit(solution)/shard_map/all_to_all | solution.py:280
  129.2 48.7 %collective-permute-start.5 = (bf16[8,2,2,32,896]{4,3,2,1,0:T(8,128)(2,1)}, bf16[8,2,2,32,896]{4,3,2,1,0:T(8,128)(2,1)}, u32[]{:S(2)}, u32[]{:S(2)}) collective-permute-start(bf16[8,2,2,32,896]{4,3,2,1,0:T(8,128)(2,1)} %all-to-all-done.2.rest_4_), channel_id=1, source_target_pairs={{0,2},{1,3},{2,0},{3,1},{4,6},{5,7},{6,4},{7,5},{8,10},{9,11},{10,... | collective-permute-start | bytes 5505032 | tf_op jit(solution)/shard_map/ppermute | solution.py:255
  130.6 47.3 %collective-permute-start.9 = (bf16[8,2,2,32,896]{4,3,2,1,0:T(8,128)(2,1)}, bf16[8,2,2,32,896]{4,3,2,1,0:T(8,128)(2,1)}, u32[]{:S(2)}, u32[]{:S(2)}) collective-permute-start(bf16[8,2,2,32,896]{4,3,2,1,0:T(8,128)(2,1)} %all-to-all-done.2.rest_4_), channel_id=1, source_target_pairs={{0,1},{1,0},{2,3},{3,2},{4,5},{5,4},{6,7},{7,6},{8,9},{9,8},{10,11... | collective-permute-start | bytes 5505032 | tf_op jit(solution)/shard_map/ppermute | solution.py:255
  130.6 47.3 %collective-permute-start.2 = (bf16[8,16,2,32,128]{4,3,2,1,0:T(8,128)(2,1)S(1)}, bf16[8,16,2,32,128]{4,3,2,1,0:T(8,128)(2,1)}, u32[]{:S(2)}, u32[]{:S(2)}) collective-permute-start(bf16[8,16,2,32,128]{4,3,2,1,0:T(8,128)(2,1)S(1)} %copy-done.2), channel_id=1, source_target_pairs={{0,1},{1,0},{2,3},{3,2},{4,5},{5,4},{6,7},{7,6},{8,9},{9,8},{10,11... | collective-permute-start | bytes 6291464 | tf_op jit(solution)/shard_map/ppermute | solution.py:255
  177.9 49.7 %all-to-all-start.4 = ((bf16[8,2,2,32,896]{4,3,2,1,0:T(8,128)(2,1)}), bf16[8,2,2,32,896]{4,3,2,1,0:T(8,128)(2,1)S(1)}, u32[]{:S(2)}, u32[]{:S(2)}) async-start(bf16[8,2,2,32,896]{4,3,2,1,0:T(8,128)(2,1)} %get-tuple-element.46), calls=%async_computation.4 | async-start | bytes 3670016 | tf_op jit(solution)/shard_map/all_to_all | solution.py:280
  183.9 41.9 %collective-permute-start.3 = (bf16[8,2,2,32,896]{4,3,2,1,0:T(8,128)(2,1)}, bf16[8,2,2,32,896]{4,3,2,1,0:T(8,128)(2,1)S(1)}, u32[]{:S(2)}, u32[]{:S(2)}) collective-permute-start(bf16[8,2,2,32,896]{4,3,2,1,0:T(8,128)(2,1)} %all-to-all-done.1.rest_4_), channel_id=1, source_target_pairs={{0,2},{1,3},{2,0},{3,1},{4,6},{5,7},{6,4},{7,5},{8,10},{9,11},{10,... | collective-permute-start | bytes 5505032 | tf_op jit(solution)/shard_map/ppermute | solution.py:255
  184.5 41.3 %collective-permute-start.4 = (bf16[8,2,2,32,896]{4,3,2,1,0:T(8,128)(2,1)}, bf16[8,2,2,32,896]{4,3,2,1,0:T(8,128)(2,1)S(1)}, u32[]{:S(2)}, u32[]{:S(2)}) collective-permute-start(bf16[8,2,2,32,896]{4,3,2,1,0:T(8,128)(2,1)} %all-to-all-done.1.rest_4_), channel_id=1, source_target_pairs={{0,1},{1,0},{2,3},{3,2},{4,5},{5,4},{6,7},{7,6},{8,9},{9,8},{10,11... | collective-permute-start | bytes 5505032 | tf_op jit(solution)/shard_map/ppermute | solution.py:255
  184.5 43.1 %collective-permute-start.6 = (bf16[8,2,2,32,896]{4,3,2,1,0:T(8,128)(2,1)}, bf16[8,2,2,32,896]{4,3,2,1,0:T(8,128)(2,1)}, u32[]{:S(2)}, u32[]{:S(2)}) collective-permute-start(bf16[8,2,2,32,896]{4,3,2,1,0:T(8,128)(2,1)} %collective-permute-done.5.rest_6_), channel_id=1, source_target_pairs={{0,1},{1,0},{2,3},{3,2},{4,5},{5,4},{6,7},{7,6},{8,9},{9,8},{10,11... | collective-permute-start | bytes 5505032 | tf_op jit(solution)/shard_map/ppermute | solution.py:255
  228.9 47.1 %all-to-all-start.3 = ((bf16[8,2,2,32,896]{4,3,2,1,0:T(8,128)(2,1)}), bf16[8,2,2,32,896]{4,3,2,1,0:T(8,128)(2,1)S(1)}, u32[]{:S(2)}, u32[]{:S(2)}) async-start(bf16[8,2,2,32,896]{4,3,2,1,0:T(8,128)(2,1)} %get-tuple-element.42), calls=%async_computation.3 | async-start | bytes 3670016 | tf_op jit(solution)/shard_map/all_to_all | solution.py:280
  234.6 40.5 %collective-permute-start.10 = (bf16[8,2,2,32,896]{4,3,2,1,0:T(8,128)(2,1)}, bf16[8,2,2,32,896]{4,3,2,1,0:T(8,128)(2,1)}, u32[]{:S(2)}, u32[]{:S(2)}) collective-permute-start(bf16[8,2,2,32,896]{4,3,2,1,0:T(8,128)(2,1)} %copy-done.6), channel_id=1, source_target_pairs={{0,2},{1,3},{2,0},{3,1},{4,6},{5,7},{6,4},{7,5},{8,10},{9,11},{10,... | collective-permute-start | bytes 5505032 | tf_op jit(solution)/shard_map/ppermute | solution.py:255
  277.3 46.3 %all-to-all-start.6 = ((bf16[8,2,2,32,896]{4,3,2,1,0:T(8,128)(2,1)}), bf16[8,2,2,32,896]{4,3,2,1,0:T(8,128)(2,1)S(1)}, u32[]{:S(2)}, u32[]{:S(2)}) async-start(bf16[8,2,2,32,896]{4,3,2,1,0:T(8,128)(2,1)} %get-tuple-element.53), calls=%async_computation.6 | async-start | bytes 3670016 | tf_op jit(solution)/shard_map/all_to_all | solution.py:280
  282.0 40.7 %collective-permute-start.7 = (bf16[8,2,2,32,896]{4,3,2,1,0:T(8,128)(2,1)}, bf16[8,2,2,32,896]{4,3,2,1,0:T(8,128)(2,1)}, u32[]{:S(2)}, u32[]{:S(2)}) collective-permute-start(bf16[8,2,2,32,896]{4,3,2,1,0:T(8,128)(2,1)} %copy-done.5), channel_id=1, source_target_pairs={{0,2},{1,3},{2,0},{3,1},{4,6},{5,7},{6,4},{7,5},{8,10},{9,11},{10,... | collective-permute-start | bytes 5505032 | tf_op jit(solution)/shard_map/ppermute | solution.py:255
  323.6 46.5 %all-to-all-start.5 = ((bf16[8,2,2,32,896]{4,3,2,1,0:T(8,128)(2,1)}), bf16[8,2,2,32,896]{4,3,2,1,0:T(8,128)(2,1)}, u32[]{:S(2)}, u32[]{:S(2)}) async-start(bf16[8,2,2,32,896]{4,3,2,1,0:T(8,128)(2,1)} %get-tuple-element.48), calls=%async_computation.5 | async-start | bytes 3670016 | tf_op jit(solution)/shard_map/all_to_all | solution.py:280
  370.1 46.4 %all-to-all-start.8 = ((bf16[8,2,2,32,896]{4,3,2,1,0:T(8,128)(2,1)}), bf16[8,2,2,32,896]{4,3,2,1,0:T(8,128)(2,1)S(1)}, u32[]{:S(2)}, u32[]{:S(2)}) async-start(bf16[8,2,2,32,896]{4,3,2,1,0:T(8,128)(2,1)} %get-tuple-element.59), calls=%async_computation.8 | async-start | bytes 3670016 | tf_op jit(solution)/shard_map/all_to_all | solution.py:280
  374.6 41.0 %collective-permute-start.13 = (bf16[8,2,2,32,896]{4,3,2,1,0:T(8,128)(2,1)}, bf16[8,2,2,32,896]{4,3,2,1,0:T(8,128)(2,1)}, u32[]{:S(2)}, u32[]{:S(2)}) collective-permute-start(bf16[8,2,2,32,896]{4,3,2,1,0:T(8,128)(2,1)} %all-to-all-done.5.rest_4_), channel_id=1, source_target_pairs={{0,2},{1,3},{2,0},{3,1},{4,6},{5,7},{6,4},{7,5},{8,10},{9,11},{10,... | collective-permute-start | bytes 5505032 | tf_op jit(solution)/shard_map/ppermute | solution.py:255
  416.4 46.6 %all-to-all-start.7 = ((bf16[8,2,2,32,896]{4,3,2,1,0:T(8,128)(2,1)}), bf16[8,2,2,32,896]{4,3,2,1,0:T(8,128)(2,1)}, u32[]{:S(2)}, u32[]{:S(2)}) async-start(bf16[8,2,2,32,896]{4,3,2,1,0:T(8,128)(2,1)} %get-tuple-element.55), calls=%async_computation.7 | async-start | bytes 3670016 | tf_op jit(solution)/shard_map/all_to_all | solution.py:280
  421.4 40.5 %collective-permute-start.23 = (bf16[8,2,2,32,896]{4,3,2,1,0:T(8,128)(2,1)S(1)}, bf16[8,2,2,32,896]{4,3,2,1,0:T(8,128)(2,1)}, u32[]{:S(2)}, u32[]{:S(2)}) collective-permute-start(bf16[8,2,2,32,896]{4,3,2,1,0:T(8,128)(2,1)S(1)} %all-to-all-done.8.rest_4_), channel_id=1, source_target_pairs={{0,2},{1,3},{2,0},{3,1},{4,6},{5,7},{6,4},{7,5},{8,10},{9,11},{10,... | collective-permute-start | bytes 5505032 | tf_op jit(solution)/shard_map/ppermute | solution.py:255
  421.9 50.2 %collective-permute-start.25 = (bf16[8,2,2,32,896]{4,3,2,1,0:T(8,128)(2,1)}, bf16[8,2,2,32,896]{4,3,2,1,0:T(8,128)(2,1)}, u32[]{:S(2)}, u32[]{:S(2)}) collective-permute-start(bf16[8,2,2,32,896]{4,3,2,1,0:T(8,128)(2,1)} %collective-permute-done.13.rest_6_), channel_id=1, source_target_pairs={{0,1},{1,0},{2,3},{3,2},{4,5},{5,4},{6,7},{7,6},{8,9},{9,8},{10,11... | collective-permute-start | bytes 5505032 | tf_op jit(solution)/shard_map/ppermute | solution.py:255
  421.9 58.8 %collective-permute-start.22 = (bf16[8,2,2,32,896]{4,3,2,1,0:T(8,128)(2,1)S(1)}, bf16[8,2,2,32,896]{4,3,2,1,0:T(8,128)(2,1)}, u32[]{:S(2)}, u32[]{:S(2)}) collective-permute-start(bf16[8,2,2,32,896]{4,3,2,1,0:T(8,128)(2,1)S(1)} %all-to-all-done.8.rest_4_), channel_id=1, source_target_pairs={{0,1},{1,0},{2,3},{3,2},{4,5},{5,4},{6,7},{7,6},{8,9},{9,8},{10,11... | collective-permute-start | bytes 5505032 | tf_op jit(solution)/shard_map/ppermute | solution.py:255
  463.0 41.6 %collective-permute-start.20 = (bf16[8,2,2,32,896]{4,3,2,1,0:T(8,128)(2,1)}, bf16[8,2,2,32,896]{4,3,2,1,0:T(8,128)(2,1)}, u32[]{:S(2)}, u32[]{:S(2)}) collective-permute-start(bf16[8,2,2,32,896]{4,3,2,1,0:T(8,128)(2,1)} %all-to-all-done.7.rest_4_), channel_id=1, source_target_pairs={{0,2},{1,3},{2,0},{3,1},{4,6},{5,7},{6,4},{7,5},{8,10},{9,11},{10,... | collective-permute-start | bytes 5505032 | tf_op jit(solution)/shard_map/ppermute | solution.py:255
  (23 other events, 500.8 us)

commit v3 on v2

--- a/solution.py
+++ b/solution.py
@@ -174,8 +174,9 @@
     )(voltages, voltages, voltages, voltages, window, table, gain_re, gain_im)
 
 
-def correlate_kernel(tiles, me_ref, *rest):
-    heads, bodies, out_ref, left_ref = rest[:tiles], rest[tiles : 2 * tiles], rest[-2], rest[-1]
+def correlate_kernel(steps, me_ref, *rest):
+    count = len(steps) + (0 not in steps)
+    heads, bodies, out_ref, left_ref = rest[:count], rest[count : 2 * count], rest[-2], rest[-1]
     rows = heads[0].shape[0] * heads[0].shape[3]
 
     def part(r, p):
@@ -188,20 +189,22 @@
     left_ref[rows:, 0:FRAMES] = im
     left_ref[rows:, FRAMES:] = -re
     factor = 1.0 / FRAMES
-    for r in range(tiles):
+    for place, step in enumerate(steps):
+        r = count - len(steps) + place
         other = jnp.concatenate([*part(r, 0), *part(r, 1)], axis=1)
         both = lax.dot_general(
             left_ref[...], other, (((1,), (1,)), ((), ())), preferred_element_type=jnp.float32
         )
-        at = pl.ds(pl.multiple_of((me_ref[0] ^ r) * rows, rows), rows)
+        column = (me_ref[0] ^ step) % len(steps)
+        at = pl.ds(pl.multiple_of(column * rows, rows), rows)
         out_ref[0, 0, :, at] = both[:rows] * factor
         out_ref[1, 0, :, at] = both[rows:] * factor
 
 
-def correlate(me, heads, bodies, previous, first, channels):
+def correlate(me, tiles, steps, heads, bodies, previous, first, channels):
     freq, size, _, owned, _ = bodies[0].shape
-    tiles = len(bodies)
     rows = freq * owned
+    width = len(steps)
     in_specs = [
         pl.BlockSpec((freq, 1, 2, owned, x.shape[-1]), lambda c, me: (0, first + c, 0, 0, 0))
         for x in heads
@@ -215,20 +218,23 @@
         aliases = {len(args): 0}
         args.append(previous)
     return pl.pallas_call(
-        functools.partial(correlate_kernel, tiles),
+        functools.partial(correlate_kernel, steps),
         grid_spec=pltpu.PrefetchScalarGridSpec(
             num_scalar_prefetch=1,
             grid=(size,),
             in_specs=in_specs,
-            out_specs=pl.BlockSpec((2, 1, rows, tiles * rows), lambda c, me: (0, first + c, 0, 0)),
+            out_specs=pl.BlockSpec(
+                (2, 1, rows, width * rows),
+                lambda c, me: (0, first + c, 0, (me[0] ^ steps[0]) // width),
+            ),
             scratch_shapes=[pltpu.VMEM((2 * rows, 2 * FRAMES), jnp.bfloat16)],
         ),
         out_shape=jax.ShapeDtypeStruct((2, channels, rows, tiles * rows), jnp.float32),
         input_output_aliases=aliases,
         compiler_params=pltpu.CompilerParams(vmem_limit_bytes=VMEM),
         cost_estimate=pl.CostEstimate(
-            flops=size * 2 * (2 * rows) * (2 * FRAMES) * (tiles * rows),
-            bytes_accessed=size * (tiles * rows * FRAMES * 4 + 2 * rows * tiles * rows * 4),
+            flops=size * 2 * (2 * rows) * (2 * FRAMES) * (width * rows),
+            bytes_accessed=size * (tiles * rows * FRAMES * 4 + 2 * rows * width * rows * 4),
             transcendentals=0,
         ),
     )(*args)
@@ -250,6 +256,10 @@
     messages += analyse(voltages, *tables, freq, 0, sizes[:lead], 1, blocks - 1)
     messages[1], again = lax.optimization_barrier((messages[1], voltages))
     messages += analyse(again, *tables, freq, sum(sizes[:lead]), sizes[lead:], 1, blocks - 1)
+    if lead > 1:
+        messages[lead], messages[lead + 1] = lax.optimization_barrier(
+            (messages[lead], messages[lead + 1])
+        )
 
     def swap(array, bit):
         return lax.ppermute(array, "tile", [(t, t ^ bit) for t in range(tile)])
@@ -258,11 +268,12 @@
     firsts = [sum(sizes[:k]) for k in range(count)]
     turned, across, beside, opposite, results = ([None] * count for _ in range(5))
 
-    def finish(k):
-        heads, bodies = (
-            [turned[m], beside[m], across[m], opposite[m]] for m in (0, k)
-        )
-        results[k] = correlate(me, heads, bodies, results[k - 1], firsts[k - 1], channels)
+    def finish(k, steps):
+        parts = (turned, beside, across, opposite)
+        wanted = steps if 0 in steps else (0, *steps)
+        heads, bodies = ([parts[step][m] for step in wanted] for m in (0, k))
+        before = results[k] if results[k] is not None else results[k - 1]
+        results[k] = correlate(me, tile, steps, heads, bodies, before, firsts[k - 1], channels)
 
     def after(array, *waits):
         waits = [w for w in waits if w is not None]
@@ -282,10 +293,11 @@
         beside[k] = swap(turned[k], 1)
         source = across[k]
         if k == count - 1:
-            source = after(source, results[k - 1])
+            finish(k, (0, 1))
+            source = after(source, results[k])
         opposite[k] = swap(source, 1)
         if k >= 1:
-            finish(k)
+            finish(k, (2, 3) if k == count - 1 else (0, 1, 2, 3))
     return results[-1]
 
 

time: 519 us -> 512 us (0.987)
  waiting for transfers between devices: 287 us -> 280 us
    ppermute x27, waiting for transfers between devices: 269 us -> 261 us  [swap(): return lax.ppermute(array, 'tile', [(t, t ^ bit) for t in range(tile)])]
    pallas_call x8 -> x9, Pallas kernels: 68.4 us -> 71 us  [correlate(): pl.pallas_call(functools.partial(correlate_kernel, steps), grid_spec=pltp...]
  transfers between devices with their start and end apart: 36 -> 36, of which waited for: 15 -> 16; matrix products, arithmetic and copies ran while one was open for 0% -> 0% of each run, Pallas kernels for 27% -> 29%
where the time goes in v3:
time: 512 us
  waiting for transfers between devices  280 us (55%)
  Pallas kernels  164 us (32%)
  starting transfers between devices  56.7 us (11%)
  local copies, waits for them, and re-layouts  7.75 us (2%)
    ppermute x27, waiting for transfers between devices, swap(): return lax.ppermute(array, 'tile', [(t, t ^ bit) for t in range(tile)])  261 us
    pallas_call x3, Pallas kernels, analyse(): pl.pallas_call(functools.partial(analyse_kernel, owned, freq, low, sizes)...  93.2 us
    pallas_call x9, Pallas kernels, correlate(): pl.pallas_call(functools.partial(correlate_kernel, steps), grid_spec=pltp...  71 us
    all_to_all x9, starting transfers between devices, per_device(): lax.all_to_all(message, 'freq', split_axis=0, concat_axis=0, tiled=True)  47.5 us
    all_to_all x9, waiting for transfers between devices, per_device(): lax.all_to_all(message, 'freq', split_axis=0, concat_axis=0, tiled=True)  18.7 us
  transfers between devices with their start and end apart: 36, of which 16 were waited for; matrix products, arithmetic and copies ran while one was open for 0% of the time, Pallas kernels for 29%

profile of v3, /device:TPU:0, one launch (start us, length us, event | category | flops | bytes accessed | tf_op | source)
XLA Modules:
  0.0 511.5 jit_solution(5184251642199495255)
XLA Ops:
  2.6 11.6 %shard_map.37 = bf16[8,16,2,32,128]{4,3,2,1,0:T(8,128)(2,1)} custom-call(bf16[32,262912]{1,0:T(8,128)(2,1)} %h2_ref.4, bf16[32,262912]{1,0:T(8,128)(2,1)} %h2_ref.4, bf16[32,262912]{1,0:T(8,128)(2,1)} %h2_ref.4, bf16[32,262912]{1,0:T(8,128)(2,1)} %h2_ref.4, f32[4,256]{1,0:T(4,128)} %fusion.11.window_ref, bf16[256,256]{1,0:T(8,128)(2,1)} %select_convert_fusion.table_ref, ...), custom_call_target="tpu_custom_call" | custom-call | flops 4294967296 | bytes 4194304 | tf_op jit(solution)/shard_map/pallas_call | solution.py:143
  14.1 7.3 %all-to-all-start = ((bf16[8,16,2,32,128]{4,3,2,1,0:T(8,128)(2,1)}), bf16[8,16,2,32,128]{4,3,2,1,0:T(8,128)(2,1)S(1)}, u32[]{:S(2)}, u32[]{:S(2)}) async-start(bf16[8,16,2,32,128]{4,3,2,1,0:T(8,128)(2,1)} %shard_map.37), calls=%async_computation | async-start | bytes 4194304 | tf_op jit(solution)/shard_map/all_to_all | solution.py:291
  21.4 34.9 %shard_map.38 = (bf16[8,2,2,32,896]{4,3,2,1,0:T(8,128)(2,1)}, bf16[8,2,2,32,896]{4,3,2,1,0:T(8,128)(2,1)}) custom-call(bf16[32,262912]{1,0:T(8,128)(2,1)} %h2_ref.4, bf16[32,262912]{1,0:T(8,128)(2,1)} %h2_ref.4, bf16[32,262912]{1,0:T(8,128)(2,1)} %h2_ref.4, bf16[32,262912]{1,0:T(8,128)(2,1)} %h2_ref.4, f32[4,256]{1,0:T(4,128)} %fusion.11.window_ref, ...), custom_call_target="tpu_custom_call" | custom-call | flops 30064771072 | bytes 29360128 | tf_op jit(solution)/shard_map/pallas_call | solution.py:143
  56.3 13.3 %all-to-all-done.rest_0_ = bf16[8,16,2,32,128]{4,3,2,1,0:T(8,128)(2,1)S(1)} async-done(((bf16[8,16,2,32,128]{4,3,2,1,0:T(8,128)(2,1)}), bf16[8,16,2,32,128]{4,3,2,1,0:T(8,128)(2,1)S(1)}, u32[]{:S(2)}, u32[]{:S(2)}) %all-to-all-start) | async-done | bytes 2097184 | tf_op jit(solution)/shard_map/all_to_all | solution.py:291
  75.5 46.8 %shard_map.39 = (bf16[8,2,2,32,896]{4,3,2,1,0:T(8,128)(2,1)}, bf16[8,2,2,32,896]{4,3,2,1,0:T(8,128)(2,1)}, bf16[8,2,2,32,896]{4,3,2,1,0:T(8,128)(2,1)}, bf16[8,2...) custom-call(bf16[32,262912]{1,0:T(8,128)(2,1)} %h2_ref.4, ...), custom_call_target="tpu_custom_call" | custom-call | flops 30064771072 | bytes 29360128 | tf_op jit(solution)/shard_map/pallas_call | solution.py:143
  122.3 5.8 %all-to-all-start.1 = ((bf16[8,2,2,32,896]{4,3,2,1,0:T(8,128)(2,1)}), bf16[8,2,2,32,896]{4,3,2,1,0:T(8,128)(2,1)}, u32[]{:S(2)}, u32[]{:S(2)}) async-start(bf16[8,2,2,32,896]{4,3,2,1,0:T(8,128)(2,1)} %get-tuple-element.43), calls=%async_computation.1 | async-start | bytes 3670016 | tf_op jit(solution)/shard_map/all_to_all | solution.py:291
  129.0 41.9 %collective-permute-done.5.rest_6_ = bf16[8,2,2,32,896]{4,3,2,1,0:T(8,128)(2,1)S(1)} collective-permute-done((bf16[8,2,2,32,896]{4,3,2,1,0:T(8,128)(2,1)}, bf16[8,2,2,32,896]{4,3,2,1,0:T(8,128)(2,1)S(1)}, u32[]{:S(2)}, u32[]{:S(2)}) %collective-permute-start.5) | collective-permute-done | bytes 1835040 | tf_op jit(solution)/shard_map/ppermute | solution.py:265
  174.8 6.0 %all-to-all-start.4 = ((bf16[8,2,2,32,896]{4,3,2,1,0:T(8,128)(2,1)}), bf16[8,2,2,32,896]{4,3,2,1,0:T(8,128)(2,1)}, u32[]{:S(2)}, u32[]{:S(2)}) async-start(bf16[8,2,2,32,896]{4,3,2,1,0:T(8,128)(2,1)} %get-tuple-element.50), calls=%async_computation.4 | async-start | bytes 3670016 | tf_op jit(solution)/shard_map/all_to_all | solution.py:291
  181.8 40.6 %collective-permute-done.3.rest_6_ = bf16[8,2,2,32,896]{4,3,2,1,0:T(8,128)(2,1)} collective-permute-done((bf16[8,2,2,32,896]{4,3,2,1,0:T(8,128)(2,1)}, bf16[8,2,2,32,896]{4,3,2,1,0:T(8,128)(2,1)}, u32[]{:S(2)}, u32[]{:S(2)}) %collective-permute-start.3) | collective-permute-done | bytes 1835040 | tf_op jit(solution)/shard_map/ppermute | solution.py:265
  229.2 8.5 %shard_map.40.rest_8_ = f32[2,16,256,1024]{3,2,1,0:T(8,128)} custom-call(s32[1]{0:T(128)} %bitcast.me_ref, bf16[8,16,2,32,128]{4,3,2,1,0:T(8,128)(2,1)} %copy-done, bf16[8,16,2,32,128]{4,3,2,1,0:T(8,128)(2,1)} %collective-permute-done.2.rest_1_, bf16[8,16,2,32,128]{4,3,2,1,0:T(8,128)(2,1)} %collective-permute-done.rest_2_.rest_1_, ...), custom_call_target="tpu_custom_call" | custom-call | flops 4294967296 | bytes 12582912 | tf_op jit(solution)/shard_map/pallas_call | solution.py:220
  237.8 31.2 %collective-permute-done.10.rest_6_ = bf16[8,2,2,32,896]{4,3,2,1,0:T(8,128)(2,1)} collective-permute-done((bf16[8,2,2,32,896]{4,3,2,1,0:T(8,128)(2,1)}, bf16[8,2,2,32,896]{4,3,2,1,0:T(8,128)(2,1)}, u32[]{:S(2)}, u32[]{:S(2)}) %collective-permute-start.10) | collective-permute-done | bytes 1835040 | tf_op jit(solution)/shard_map/ppermute | solution.py:265
  277.0 8.6 %shard_map.41.rest_8_ = f32[2,16,256,1024]{3,2,1,0:T(8,128)} custom-call(s32[1]{0:T(128)} %bitcast.me_ref, bf16[8,16,2,32,128]{4,3,2,1,0:T(8,128)(2,1)} %copy-done, bf16[8,16,2,32,128]{4,3,2,1,0:T(8,128)(2,1)} %collective-permute-done.2.rest_1_, bf16[8,16,2,32,128]{4,3,2,1,0:T(8,128)(2,1)} %collective-permute-done.rest_2_.rest_1_, ...), custom_call_target="tpu_custom_call", output_to_operand_aliasing={{}: (9, {})} | custom-call | flops 4294967296 | bytes 12582912 | tf_op jit(solution)/shard_map/pallas_call | solution.py:220
  285.6 31.1 %collective-permute-done.7.rest_6_ = bf16[8,2,2,32,896]{4,3,2,1,0:T(8,128)(2,1)} collective-permute-done((bf16[8,2,2,32,896]{4,3,2,1,0:T(8,128)(2,1)}, bf16[8,2,2,32,896]{4,3,2,1,0:T(8,128)(2,1)}, u32[]{:S(2)}, u32[]{:S(2)}) %collective-permute-start.7) | collective-permute-done | bytes 1835040 | tf_op jit(solution)/shard_map/ppermute | solution.py:265
  323.5 8.6 %shard_map.42.rest_8_ = f32[2,16,256,1024]{3,2,1,0:T(8,128)} custom-call(s32[1]{0:T(128)} %bitcast.me_ref, bf16[8,16,2,32,128]{4,3,2,1,0:T(8,128)(2,1)} %copy-done, bf16[8,16,2,32,128]{4,3,2,1,0:T(8,128)(2,1)} %collective-permute-done.2.rest_1_, bf16[8,16,2,32,128]{4,3,2,1,0:T(8,128)(2,1)} %collective-permute-done.rest_2_.rest_1_, ...), custom_call_target="tpu_custom_call", output_to_operand_aliasing={{}: (9, {})} | custom-call | flops 4294967296 | bytes 12582912 | tf_op jit(solution)/shard_map/pallas_call | solution.py:220
  332.0 30.8 %collective-permute-done.16.rest_6_ = bf16[8,2,2,32,896]{4,3,2,1,0:T(8,128)(2,1)} collective-permute-done((bf16[8,2,2,32,896]{4,3,2,1,0:T(8,128)(2,1)S(1)}, bf16[8,2,2,32,896]{4,3,2,1,0:T(8,128)(2,1)}, u32[]{:S(2)}, u32[]{:S(2)}) %collective-permute-start.16) | collective-permute-done | bytes 1835040 | tf_op jit(solution)/shard_map/ppermute | solution.py:265
  369.7 8.6 %shard_map.43.rest_8_ = f32[2,16,256,1024]{3,2,1,0:T(8,128)} custom-call(s32[1]{0:T(128)} %bitcast.me_ref, bf16[8,16,2,32,128]{4,3,2,1,0:T(8,128)(2,1)} %copy-done, bf16[8,16,2,32,128]{4,3,2,1,0:T(8,128)(2,1)} %collective-permute-done.2.rest_1_, bf16[8,16,2,32,128]{4,3,2,1,0:T(8,128)(2,1)} %collective-permute-done.rest_2_.rest_1_, ...), custom_call_target="tpu_custom_call", output_to_operand_aliasing={{}: (9, {})} | custom-call | flops 4294967296 | bytes 12582912 | tf_op jit(solution)/shard_map/pallas_call | solution.py:220
  378.2 31.3 %collective-permute-done.13.rest_6_ = bf16[8,2,2,32,896]{4,3,2,1,0:T(8,128)(2,1)} collective-permute-done((bf16[8,2,2,32,896]{4,3,2,1,0:T(8,128)(2,1)}, bf16[8,2,2,32,896]{4,3,2,1,0:T(8,128)(2,1)}, u32[]{:S(2)}, u32[]{:S(2)}) %collective-permute-start.13) | collective-permute-done | bytes 1835040 | tf_op jit(solution)/shard_map/ppermute | solution.py:265
  417.6 39.7 %collective-permute-done.23.rest_6_ = bf16[8,2,2,32,896]{4,3,2,1,0:T(8,128)(2,1)} collective-permute-done((bf16[8,2,2,32,896]{4,3,2,1,0:T(8,128)(2,1)}, bf16[8,2,2,32,896]{4,3,2,1,0:T(8,128)(2,1)}, u32[]{:S(2)}, u32[]{:S(2)}) %collective-permute-start.23) | collective-permute-done | bytes 1835040 | tf_op jit(solution)/shard_map/ppermute | solution.py:265
  458.7 8.6 %shard_map.44.rest_8_ = f32[2,16,256,1024]{3,2,1,0:T(8,128)} custom-call(s32[1]{0:T(128)} %bitcast.me_ref, bf16[8,16,2,32,128]{4,3,2,1,0:T(8,128)(2,1)} %copy-done, bf16[8,16,2,32,128]{4,3,2,1,0:T(8,128)(2,1)} %collective-permute-done.2.rest_1_, bf16[8,16,2,32,128]{4,3,2,1,0:T(8,128)(2,1)} %collective-permute-done.rest_2_.rest_1_, ...), custom_call_target="tpu_custom_call", output_to_operand_aliasing={{}: (9, {})} | custom-call | flops 4294967296 | bytes 12582912 | tf_op jit(solution)/shard_map/pallas_call | solution.py:220
  467.3 8.6 %shard_map.45.rest_8_ = f32[2,16,256,1024]{3,2,1,0:T(8,128)} custom-call(s32[1]{0:T(128)} %bitcast.me_ref, bf16[8,16,2,32,128]{4,3,2,1,0:T(8,128)(2,1)} %copy-done, bf16[8,16,2,32,128]{4,3,2,1,0:T(8,128)(2,1)} %collective-permute-done.2.rest_1_, bf16[8,16,2,32,128]{4,3,2,1,0:T(8,128)(2,1)} %collective-permute-done.rest_2_.rest_1_, ...), custom_call_target="tpu_custom_call", output_to_operand_aliasing={{}: (9, {})} | custom-call | flops 4294967296 | bytes 12582912 | tf_op jit(solution)/shard_map/pallas_call | solution.py:220
  475.9 8.6 %shard_map.46.rest_4_ = f32[2,16,256,1024]{3,2,1,0:T(8,128)} custom-call(s32[1]{0:T(128)} %bitcast.me_ref, bf16[8,16,2,32,128]{4,3,2,1,0:T(8,128)(2,1)} %copy-done, bf16[8,16,2,32,128]{4,3,2,1,0:T(8,128)(2,1)} %collective-permute-done.2.rest_1_, bf16[8,16,2,32,128]{4,3,2,1,0:T(8,128)(2,1)} %collective-permute-done.rest_2_.rest_1_, ...), custom_call_target="tpu_custom_call", output_to_operand_aliasing={{}: (9, {})} | custom-call | flops 4294967296 | bytes 12582912 | tf_op jit(solution)/shard_map/pallas_call | solution.py:220
  484.5 5.3 %shard_map.47.rest_6_ = f32[2,16,256,1024]{3,2,1,0:T(8,128)} custom-call(s32[1]{0:T(128)} %bitcast.me_ref, bf16[8,16,2,32,128]{4,3,2,1,0:T(8,128)(2,1)} %copy-done, bf16[8,16,2,32,128]{4,3,2,1,0:T(8,128)(2,1)} %collective-permute-done.2.rest_1_, bf16[8,2,2,32,896]{4,3,2,1,0:T(8,128)(2,1)} %copy-done.2, ...), custom_call_target="tpu_custom_call", output_to_operand_aliasing={{}: (5, {})} | custom-call | flops 2147483648 | bytes 10485760 | tf_op jit(solution)/shard_map/pallas_call | solution.py:220
  489.8 10.8 %collective-permute-done.19.rest_4_ = bf16[8,2,2,32,896]{4,3,2,1,0:T(8,128)(2,1)} collective-permute-done((bf16[8,2,2,32,896]{4,3,2,1,0:T(8,128)(2,1)S(1)}, bf16[8,2,2,32,896]{4,3,2,1,0:T(8,128)(2,1)}, u32[]{:S(2)}, u32[]{:S(2)}) %collective-permute-start.19) | collective-permute-done | bytes 1835040 | tf_op jit(solution)/shard_map/ppermute | solution.py:265
  505.9 5.6 %shard_map.48 = f32[2,16,256,1024]{3,2,1,0:T(8,128)} custom-call(s32[1]{0:T(128)} %bitcast.me_ref, bf16[8,16,2,32,128]{4,3,2,1,0:T(8,128)(2,1)} %copy-done, bf16[8,16,2,32,128]{4,3,2,1,0:T(8,128)(2,1)} %collective-permute-done.rest_2_.rest_1_, bf16[8,16,2,32,128]{4,3,2,1,0:T(8,128)(2,1)} %copy-done.1, ...), custom_call_target="tpu_custom_call", output_to_operand_aliasing={{}: (7, {})} | custom-call | flops 2147483648 | bytes 10485760 | tf_op jit(solution)/shard_map/pallas_call | solution.py:220
  (82 shorter events, 57.4 us)
Async XLA Ops:
  14.1 55.5 %all-to-all-start = ((bf16[8,16,2,32,128]{4,3,2,1,0:T(8,128)(2,1)}), bf16[8,16,2,32,128]{4,3,2,1,0:T(8,128)(2,1)S(1)}, u32[]{:S(2)}, u32[]{:S(2)}) async-start(bf16[8,16,2,32,128]{4,3,2,1,0:T(8,128)(2,1)} %shard_map.37), calls=%async_computation | async-start | bytes 4194304 | tf_op jit(solution)/shard_map/all_to_all | solution.py:291
  69.7 52.7 %all-to-all-start.2 = ((bf16[8,2,2,32,896]{4,3,2,1,0:T(8,128)(2,1)}), bf16[8,2,2,32,896]{4,3,2,1,0:T(8,128)(2,1)}, u32[]{:S(2)}, u32[]{:S(2)}) async-start(bf16[8,2,2,32,896]{4,3,2,1,0:T(8,128)(2,1)} %get-tuple-element.45), calls=%async_computation.2 | async-start | bytes 3670016 | tf_op jit(solution)/shard_map/all_to_all | solution.py:291
  74.0 48.3 %collective-permute-start = (bf16[8,16,2,32,128]{4,3,2,1,0:T(8,128)(2,1)S(1)}, bf16[8,16,2,32,128]{4,3,2,1,0:T(8,128)(2,1)}, u32[]{:S(2)}, u32[]{:S(2)}) collective-permute-start(bf16[8,16,2,32,128]{4,3,2,1,0:T(8,128)(2,1)S(1)} %all-to-all-done.rest_0_), channel_id=1, source_target_pairs={{0,2},{1,3},{2,0},{3,1},{4,6},{5,7},{6,4},{7,5},{8,10},{9,11},{10,... | collective-permute-start | bytes 6291464 | tf_op jit(solution)/shard_map/ppermute | solution.py:265
  75.5 46.8 %collective-permute-start.2 = (bf16[8,16,2,32,128]{4,3,2,1,0:T(8,128)(2,1)S(1)}, bf16[8,16,2,32,128]{4,3,2,1,0:T(8,128)(2,1)}, u32[]{:S(2)}, u32[]{:S(2)}) collective-permute-start(bf16[8,16,2,32,128]{4,3,2,1,0:T(8,128)(2,1)S(1)} %all-to-all-done.rest_0_), channel_id=1, source_target_pairs={{0,1},{1,0},{2,3},{3,2},{4,5},{5,4},{6,7},{7,6},{8,9},{9,8},{10,11... | collective-permute-start | bytes 6291464 | tf_op jit(solution)/shard_map/ppermute | solution.py:265
  122.3 51.1 %all-to-all-start.1 = ((bf16[8,2,2,32,896]{4,3,2,1,0:T(8,128)(2,1)}), bf16[8,2,2,32,896]{4,3,2,1,0:T(8,128)(2,1)}, u32[]{:S(2)}, u32[]{:S(2)}) async-start(bf16[8,2,2,32,896]{4,3,2,1,0:T(8,128)(2,1)} %get-tuple-element.43), calls=%async_computation.1 | async-start | bytes 3670016 | tf_op jit(solution)/shard_map/all_to_all | solution.py:291
  128.2 45.2 %collective-permute-start.1 = (bf16[8,16,2,32,128]{4,3,2,1,0:T(8,128)(2,1)}, bf16[8,16,2,32,128]{4,3,2,1,0:T(8,128)(2,1)S(1)}, u32[]{:S(2)}, u32[]{:S(2)}) collective-permute-start(bf16[8,16,2,32,128]{4,3,2,1,0:T(8,128)(2,1)} %collective-permute-done.rest_2_.rest_1_), channel_id=1, source_target_pairs={{0,1},{1,0},{2,3},{3,2},{4,5},{5,4},{6,7},{7,6},{8,9},{9,8},{10,11... | collective-permute-start | bytes 6291464 | tf_op jit(solution)/shard_map/ppermute | solution.py:265
  128.4 42.4 %collective-permute-start.5 = (bf16[8,2,2,32,896]{4,3,2,1,0:T(8,128)(2,1)}, bf16[8,2,2,32,896]{4,3,2,1,0:T(8,128)(2,1)S(1)}, u32[]{:S(2)}, u32[]{:S(2)}) collective-permute-start(bf16[8,2,2,32,896]{4,3,2,1,0:T(8,128)(2,1)} %all-to-all-done.2.rest_4_), channel_id=1, source_target_pairs={{0,2},{1,3},{2,0},{3,1},{4,6},{5,7},{6,4},{7,5},{8,10},{9,11},{10,... | collective-permute-start | bytes 5505032 | tf_op jit(solution)/shard_map/ppermute | solution.py:265
  128.9 43.1 %collective-permute-start.9 = (bf16[8,2,2,32,896]{4,3,2,1,0:T(8,128)(2,1)}, bf16[8,2,2,32,896]{4,3,2,1,0:T(8,128)(2,1)S(1)}, u32[]{:S(2)}, u32[]{:S(2)}) collective-permute-start(bf16[8,2,2,32,896]{4,3,2,1,0:T(8,128)(2,1)} %all-to-all-done.2.rest_4_), channel_id=1, source_target_pairs={{0,1},{1,0},{2,3},{3,2},{4,5},{5,4},{6,7},{7,6},{8,9},{9,8},{10,11... | collective-permute-start | bytes 5505032 | tf_op jit(solution)/shard_map/ppermute | solution.py:265
  174.8 48.6 %all-to-all-start.4 = ((bf16[8,2,2,32,896]{4,3,2,1,0:T(8,128)(2,1)}), bf16[8,2,2,32,896]{4,3,2,1,0:T(8,128)(2,1)}, u32[]{:S(2)}, u32[]{:S(2)}) async-start(bf16[8,2,2,32,896]{4,3,2,1,0:T(8,128)(2,1)} %get-tuple-element.50), calls=%async_computation.4 | async-start | bytes 3670016 | tf_op jit(solution)/shard_map/all_to_all | solution.py:291
  180.8 41.7 %collective-permute-start.3 = (bf16[8,2,2,32,896]{4,3,2,1,0:T(8,128)(2,1)}, bf16[8,2,2,32,896]{4,3,2,1,0:T(8,128)(2,1)}, u32[]{:S(2)}, u32[]{:S(2)}) collective-permute-start(bf16[8,2,2,32,896]{4,3,2,1,0:T(8,128)(2,1)} %all-to-all-done.1.rest_4_), channel_id=1, source_target_pairs={{0,2},{1,3},{2,0},{3,1},{4,6},{5,7},{6,4},{7,5},{8,10},{9,11},{10,... | collective-permute-start | bytes 5505032 | tf_op jit(solution)/shard_map/ppermute | solution.py:265
  181.3 41.1 %collective-permute-start.4 = (bf16[8,2,2,32,896]{4,3,2,1,0:T(8,128)(2,1)}, bf16[8,2,2,32,896]{4,3,2,1,0:T(8,128)(2,1)}, u32[]{:S(2)}, u32[]{:S(2)}) collective-permute-start(bf16[8,2,2,32,896]{4,3,2,1,0:T(8,128)(2,1)} %all-to-all-done.1.rest_4_), channel_id=1, source_target_pairs={{0,1},{1,0},{2,3},{3,2},{4,5},{5,4},{6,7},{7,6},{8,9},{9,8},{10,11... | collective-permute-start | bytes 5505032 | tf_op jit(solution)/shard_map/ppermute | solution.py:265
  181.3 41.1 %collective-permute-start.6 = (bf16[8,2,2,32,896]{4,3,2,1,0:T(8,128)(2,1)}, bf16[8,2,2,32,896]{4,3,2,1,0:T(8,128)(2,1)}, u32[]{:S(2)}, u32[]{:S(2)}) collective-permute-start(bf16[8,2,2,32,896]{4,3,2,1,0:T(8,128)(2,1)} %copy-done.6), channel_id=1, source_target_pairs={{0,1},{1,0},{2,3},{3,2},{4,5},{5,4},{6,7},{7,6},{8,9},{9,8},{10,11... | collective-permute-start | bytes 5505032 | tf_op jit(solution)/shard_map/ppermute | solution.py:265
  223.4 46.4 %all-to-all-start.3 = ((bf16[8,2,2,32,896]{4,3,2,1,0:T(8,128)(2,1)}), bf16[8,2,2,32,896]{4,3,2,1,0:T(8,128)(2,1)S(1)}, u32[]{:S(2)}, u32[]{:S(2)}) async-start(bf16[8,2,2,32,896]{4,3,2,1,0:T(8,128)(2,1)} %get-tuple-element.46), calls=%async_computation.3 | async-start | bytes 3670016 | tf_op jit(solution)/shard_map/all_to_all | solution.py:291
  228.2 40.8 %collective-permute-start.10 = (bf16[8,2,2,32,896]{4,3,2,1,0:T(8,128)(2,1)}, bf16[8,2,2,32,896]{4,3,2,1,0:T(8,128)(2,1)}, u32[]{:S(2)}, u32[]{:S(2)}) collective-permute-start(bf16[8,2,2,32,896]{4,3,2,1,0:T(8,128)(2,1)} %all-to-all-done.4.rest_4_), channel_id=1, source_target_pairs={{0,2},{1,3},{2,0},{3,1},{4,6},{5,7},{6,4},{7,5},{8,10},{9,11},{10,... | collective-permute-start | bytes 5505032 | tf_op jit(solution)/shard_map/ppermute | solution.py:265
  271.1 46.4 %all-to-all-start.6 = ((bf16[8,2,2,32,896]{4,3,2,1,0:T(8,128)(2,1)}), bf16[8,2,2,32,896]{4,3,2,1,0:T(8,128)(2,1)S(1)}, u32[]{:S(2)}, u32[]{:S(2)}) async-start(bf16[8,2,2,32,896]{4,3,2,1,0:T(8,128)(2,1)} %get-tuple-element.57), calls=%async_computation.6 | async-start | bytes 3670016 | tf_op jit(solution)/shard_map/all_to_all | solution.py:291
  276.0 40.7 %collective-permute-start.7 = (bf16[8,2,2,32,896]{4,3,2,1,0:T(8,128)(2,1)}, bf16[8,2,2,32,896]{4,3,2,1,0:T(8,128)(2,1)}, u32[]{:S(2)}, u32[]{:S(2)}) collective-permute-start(bf16[8,2,2,32,896]{4,3,2,1,0:T(8,128)(2,1)} %copy-done.4), channel_id=1, source_target_pairs={{0,2},{1,3},{2,0},{3,1},{4,6},{5,7},{6,4},{7,5},{8,10},{9,11},{10,... | collective-permute-start | bytes 5505032 | tf_op jit(solution)/shard_map/ppermute | solution.py:265
  317.5 46.5 %all-to-all-start.5 = ((bf16[8,2,2,32,896]{4,3,2,1,0:T(8,128)(2,1)}), bf16[8,2,2,32,896]{4,3,2,1,0:T(8,128)(2,1)}, u32[]{:S(2)}, u32[]{:S(2)}) async-start(bf16[8,2,2,32,896]{4,3,2,1,0:T(8,128)(2,1)} %get-tuple-element.52), calls=%async_computation.5 | async-start | bytes 3670016 | tf_op jit(solution)/shard_map/all_to_all | solution.py:291
  364.0 46.4 %all-to-all-start.8 = ((bf16[8,2,2,32,896]{4,3,2,1,0:T(8,128)(2,1)}), bf16[8,2,2,32,896]{4,3,2,1,0:T(8,128)(2,1)S(1)}, u32[]{:S(2)}, u32[]{:S(2)}) async-start(bf16[8,2,2,32,896]{4,3,2,1,0:T(8,128)(2,1)} %get-tuple-element.63), calls=%async_computation.8 | async-start | bytes 3670016 | tf_op jit(solution)/shard_map/all_to_all | solution.py:291
  368.6 41.0 %collective-permute-start.13 = (bf16[8,2,2,32,896]{4,3,2,1,0:T(8,128)(2,1)}, bf16[8,2,2,32,896]{4,3,2,1,0:T(8,128)(2,1)}, u32[]{:S(2)}, u32[]{:S(2)}) collective-permute-start(bf16[8,2,2,32,896]{4,3,2,1,0:T(8,128)(2,1)} %all-to-all-done.5.rest_4_), channel_id=1, source_target_pairs={{0,2},{1,3},{2,0},{3,1},{4,6},{5,7},{6,4},{7,5},{8,10},{9,11},{10,... | collective-permute-start | bytes 5505032 | tf_op jit(solution)/shard_map/ppermute | solution.py:265
  411.7 46.4 %all-to-all-start.7 = ((bf16[8,2,2,32,896]{4,3,2,1,0:T(8,128)(2,1)}), bf16[8,2,2,32,896]{4,3,2,1,0:T(8,128)(2,1)S(1)}, u32[]{:S(2)}, u32[]{:S(2)}) async-start(bf16[8,2,2,32,896]{4,3,2,1,0:T(8,128)(2,1)} %get-tuple-element.59), calls=%async_computation.7 | async-start | bytes 3670016 | tf_op jit(solution)/shard_map/all_to_all | solution.py:291
  416.6 40.7 %collective-permute-start.23 = (bf16[8,2,2,32,896]{4,3,2,1,0:T(8,128)(2,1)}, bf16[8,2,2,32,896]{4,3,2,1,0:T(8,128)(2,1)}, u32[]{:S(2)}, u32[]{:S(2)}) collective-permute-start(bf16[8,2,2,32,896]{4,3,2,1,0:T(8,128)(2,1)} %copy-done.5), channel_id=1, source_target_pairs={{0,2},{1,3},{2,0},{3,1},{4,6},{5,7},{6,4},{7,5},{8,10},{9,11},{10,... | collective-permute-start | bytes 5505032 | tf_op jit(solution)/shard_map/ppermute | solution.py:265
  417.1 50.2 %collective-permute-start.25 = (bf16[8,2,2,32,896]{4,3,2,1,0:T(8,128)(2,1)}, bf16[8,2,2,32,896]{4,3,2,1,0:T(8,128)(2,1)}, u32[]{:S(2)}, u32[]{:S(2)}) collective-permute-start(bf16[8,2,2,32,896]{4,3,2,1,0:T(8,128)(2,1)} %collective-permute-done.13.rest_6_), channel_id=1, source_target_pairs={{0,1},{1,0},{2,3},{3,2},{4,5},{5,4},{6,7},{7,6},{8,9},{9,8},{10,11... | collective-permute-start | bytes 5505032 | tf_op jit(solution)/shard_map/ppermute | solution.py:265
  417.1 58.8 %collective-permute-start.22 = (bf16[8,2,2,32,896]{4,3,2,1,0:T(8,128)(2,1)}, bf16[8,2,2,32,896]{4,3,2,1,0:T(8,128)(2,1)}, u32[]{:S(2)}, u32[]{:S(2)}) collective-permute-start(bf16[8,2,2,32,896]{4,3,2,1,0:T(8,128)(2,1)} %copy-done.5), channel_id=1, source_target_pairs={{0,1},{1,0},{2,3},{3,2},{4,5},{5,4},{6,7},{7,6},{8,9},{9,8},{10,11... | collective-permute-start | bytes 5505032 | tf_op jit(solution)/shard_map/ppermute | solution.py:265
  458.1 42.5 %collective-permute-start.19 = (bf16[8,2,2,32,896]{4,3,2,1,0:T(8,128)(2,1)S(1)}, bf16[8,2,2,32,896]{4,3,2,1,0:T(8,128)(2,1)}, u32[]{:S(2)}, u32[]{:S(2)}) collective-permute-start(bf16[8,2,2,32,896]{4,3,2,1,0:T(8,128)(2,1)S(1)} %all-to-all-done.7.rest_2_.rest_3_), channel_id=1, source_target_pairs={{0,2},{1,3},{2,0},{3,1},{4,6},{5,7},{6,4},{7,5},{8,10},{9,11},{10,... | collective-permute-start | bytes 5505032 | tf_op jit(solution)/shard_map/ppermute | solution.py:265
  (21 other events, 448.3 us)

commit v4 on v3

--- a/solution.py
+++ b/solution.py
@@ -42,7 +42,7 @@
 
 def chunk_sizes(channels):
     if channels == 16:
-        return (2, 2, 2, 2, 2, 2, 2, 2)
+        return (2, 2, 2, 2, 2, 2, 2, 1, 1)
     return (1,) * channels
 
 
@@ -231,7 +231,7 @@
         ),
         out_shape=jax.ShapeDtypeStruct((2, channels, rows, tiles * rows), jnp.float32),
         input_output_aliases=aliases,
-        compiler_params=pltpu.CompilerParams(vmem_limit_bytes=VMEM),
+        compiler_params=pltpu.CompilerParams(vmem_limit_bytes=VMEM // 2),
         cost_estimate=pl.CostEstimate(
             flops=size * 2 * (2 * rows) * (2 * FRAMES) * (width * rows),
             bytes_accessed=size * (tiles * rows * FRAMES * 4 + 2 * rows * width * rows * 4),

time: 512 us -> 526 us (1.027); the launches traced: 512 us -> 519 us
  waiting for transfers between devices: 280 us -> 253 us
  local copies, waits for them, and re-layouts: 7.75 us -> 33.8 us
  starting transfers between devices: 56.7 us -> 66.5 us
    unnamed x18 -> x50, local copies, waits for them, and re-layouts: 7.75 us -> 33.8 us
    ppermute x27 -> x30, waiting for transfers between devices: 261 us -> 238 us  [swap(): return lax.ppermute(array, 'tile', [(t, t ^ bit) for t in range(tile)])]
    all_to_all x9 -> x10, starting transfers between devices: 47.5 us -> 56.6 us  [per_device(): lax.all_to_all(message, 'freq', split_axis=0, concat_axis=0, tiled=True)]
    all_to_all x9 -> x10, waiting for transfers between devices: 18.7 us -> 15.4 us  [per_device(): lax.all_to_all(message, 'freq', split_axis=0, concat_axis=0, tiled=True)]
    pallas_call x9 -> x10, Pallas kernels: 71 us -> 69 us  [correlate(): pl.pallas_call(functools.partial(correlate_kernel, steps), grid_spec=pltp...]
  transfers between devices with their start and end apart: 36 -> 40, of which waited for: 16 -> 12; matrix products, arithmetic and copies ran while one was open for 0% -> 0% of each run, Pallas kernels for 29% -> 28%
where the time goes in v4:
time: 526 us; the launch traced here: 519 us
  waiting for transfers between devices  253 us (48%)
  Pallas kernels  162 us (31%)
  starting transfers between devices  66.5 us (13%)
  local copies, waits for them, and re-layouts  33.8 us (6%)
    ppermute x30, waiting for transfers between devices, swap(): return lax.ppermute(array, 'tile', [(t, t ^ bit) for t in range(tile)])  238 us
    pallas_call x3, Pallas kernels, analyse(): pl.pallas_call(functools.partial(analyse_kernel, owned, freq, low, sizes)...  93.3 us
    pallas_call x10, Pallas kernels, correlate(): pl.pallas_call(functools.partial(correlate_kernel, steps), grid_spec=pltp...  69 us
    all_to_all x10, starting transfers between devices, per_device(): lax.all_to_all(message, 'freq', split_axis=0, concat_axis=0, tiled=True)  56.6 us
    unnamed x50, local copies, waits for them, and re-layouts  33.8 us
    all_to_all x10, waiting for transfers between devices, per_device(): lax.all_to_all(message, 'freq', split_axis=0, concat_axis=0, tiled=True)  15.4 us
  transfers between devices with their start and end apart: 40, of which 12 were waited for; matrix products, arithmetic and copies ran while one was open for 0% of the time, Pallas kernels for 28%

profile of v4, /device:TPU:0, one launch (start us, length us, event | category | flops | bytes accessed | tf_op | source)
XLA Modules:
  0.0 519.0 jit_solution(2663149386649816256)
XLA Ops:
  2.6 11.6 %shard_map.37 = bf16[8,16,2,32,128]{4,3,2,1,0:T(8,128)(2,1)} custom-call(bf16[32,262912]{1,0:T(8,128)(2,1)} %h2_ref.4, bf16[32,262912]{1,0:T(8,128)(2,1)} %h2_ref.4, bf16[32,262912]{1,0:T(8,128)(2,1)} %h2_ref.4, bf16[32,262912]{1,0:T(8,128)(2,1)} %h2_ref.4, f32[4,256]{1,0:T(4,128)} %fusion.11.window_ref, bf16[256,256]{1,0:T(8,128)(2,1)} %select_convert_fusion.table_ref, ...), custom_call_target="tpu_custom_call" | custom-call | flops 4294967296 | bytes 4194304 | tf_op jit(solution)/shard_map/pallas_call | solution.py:143
  14.1 7.5 %all-to-all-start = ((bf16[8,16,2,32,128]{4,3,2,1,0:T(8,128)(2,1)}), bf16[8,16,2,32,128]{4,3,2,1,0:T(8,128)(2,1)S(1)}, u32[]{:S(2)}, u32[]{:S(2)}) async-start(bf16[8,16,2,32,128]{4,3,2,1,0:T(8,128)(2,1)} %shard_map.37), calls=%async_computation | async-start | bytes 4194304 | tf_op jit(solution)/shard_map/all_to_all | solution.py:291
  21.6 34.9 %shard_map.38 = (bf16[8,2,2,32,896]{4,3,2,1,0:T(8,128)(2,1)}, bf16[8,2,2,32,896]{4,3,2,1,0:T(8,128)(2,1)}) custom-call(bf16[32,262912]{1,0:T(8,128)(2,1)} %h2_ref.4, bf16[32,262912]{1,0:T(8,128)(2,1)} %h2_ref.4, bf16[32,262912]{1,0:T(8,128)(2,1)} %h2_ref.4, bf16[32,262912]{1,0:T(8,128)(2,1)} %h2_ref.4, f32[4,256]{1,0:T(4,128)} %fusion.11.window_ref, ...), custom_call_target="tpu_custom_call" | custom-call | flops 30064771072 | bytes 29360128 | tf_op jit(solution)/shard_map/pallas_call | solution.py:143
  56.6 13.2 %all-to-all-done.rest_0_ = bf16[8,16,2,32,128]{4,3,2,1,0:T(8,128)(2,1)S(1)} async-done(((bf16[8,16,2,32,128]{4,3,2,1,0:T(8,128)(2,1)}), bf16[8,16,2,32,128]{4,3,2,1,0:T(8,128)(2,1)S(1)}, u32[]{:S(2)}, u32[]{:S(2)}) %all-to-all-start) | async-done | bytes 2097184 | tf_op jit(solution)/shard_map/all_to_all | solution.py:291
  75.7 46.8 %shard_map.39 = (bf16[8,2,2,32,896]{4,3,2,1,0:T(8,128)(2,1)}, bf16[8,2,2,32,896]{4,3,2,1,0:T(8,128)(2,1)}, bf16[8,2,2,32,896]{4,3,2,1,0:T(8,128)(2,1)}, bf16[8,2...) custom-call(bf16[32,262912]{1,0:T(8,128)(2,1)} %h2_ref.4, ...), custom_call_target="tpu_custom_call" | custom-call | flops 30064771072 | bytes 29360128 | tf_op jit(solution)/shard_map/pallas_call | solution.py:143
  122.5 5.9 %all-to-all-start.3 = ((bf16[8,2,2,32,896]{4,3,2,1,0:T(8,128)(2,1)}), bf16[8,2,2,32,896]{4,3,2,1,0:T(8,128)(2,1)}, u32[]{:S(2)}, u32[]{:S(2)}) async-start(bf16[8,2,2,32,896]{4,3,2,1,0:T(8,128)(2,1)} %get-tuple-element.52), calls=%async_computation.3 | async-start | bytes 3670016 | tf_op jit(solution)/shard_map/all_to_all | solution.py:291
  129.1 41.9 %collective-permute-done.2.rest_6_ = bf16[8,2,2,32,896]{4,3,2,1,0:T(8,128)(2,1)S(1)} collective-permute-done((bf16[8,2,2,32,896]{4,3,2,1,0:T(8,128)(2,1)}, bf16[8,2,2,32,896]{4,3,2,1,0:T(8,128)(2,1)S(1)}, u32[]{:S(2)}, u32[]{:S(2)}) %collective-permute-start.2) | collective-permute-done | bytes 1835040 | tf_op jit(solution)/shard_map/ppermute | solution.py:265
  174.9 6.0 %all-to-all-start.2 = ((bf16[8,2,2,32,896]{4,3,2,1,0:T(8,128)(2,1)}), bf16[8,2,2,32,896]{4,3,2,1,0:T(8,128)(2,1)}, u32[]{:S(2)}, u32[]{:S(2)}) async-start(bf16[8,2,2,32,896]{4,3,2,1,0:T(8,128)(2,1)} %get-tuple-element.49), calls=%async_computation.2 | async-start | bytes 3670016 | tf_op jit(solution)/shard_map/all_to_all | solution.py:291
  181.9 40.6 %collective-permute-done.7.rest_6_ = bf16[8,2,2,32,896]{4,3,2,1,0:T(8,128)(2,1)} collective-permute-done((bf16[8,2,2,32,896]{4,3,2,1,0:T(8,128)(2,1)}, bf16[8,2,2,32,896]{4,3,2,1,0:T(8,128)(2,1)}, u32[]{:S(2)}, u32[]{:S(2)}) %collective-permute-start.7) | collective-permute-done | bytes 1835040 | tf_op jit(solution)/shard_map/ppermute | solution.py:265
  225.1 6.0 %all-to-all-start.5 = ((bf16[8,2,2,32,896]{4,3,2,1,0:T(8,128)(2,1)}), bf16[8,2,2,32,896]{4,3,2,1,0:T(8,128)(2,1)}, u32[]{:S(2)}, u32[]{:S(2)}) async-start(bf16[8,2,2,32,896]{4,3,2,1,0:T(8,128)(2,1)} %get-tuple-element.58), calls=%async_computation.5 | async-start | bytes 3670016 | tf_op jit(solution)/shard_map/all_to_all | solution.py:291
  238.2 7.6 %shard_map.40.rest_8_ = f32[2,16,256,1024]{3,2,1,0:T(8,128)} custom-call(s32[1]{0:T(128)} %bitcast.me_ref, bf16[8,16,2,32,128]{4,3,2,1,0:T(8,128)(2,1)S(1)} %all-to-all-done.rest_0_, bf16[8,16,2,32,128]{4,3,2,1,0:T(8,128)(2,1)} %collective-permute-done.6.rest_1_, bf16[8,16,2,32,128]{4,3,2,1,0:T(8,128)(2,1)} %collective-permute-done.rest_2_.rest_1_, ...), custom_call_target="tpu_custom_call" | custom-call | flops 4294967296 | bytes 12582912 | tf_op jit(solution)/shard_map/pallas_call | solution.py:220
  245.9 25.5 %collective-permute-done.4.rest_6_ = bf16[8,2,2,32,896]{4,3,2,1,0:T(8,128)(2,1)} collective-permute-done((bf16[8,2,2,32,896]{4,3,2,1,0:T(8,128)(2,1)}, bf16[8,2,2,32,896]{4,3,2,1,0:T(8,128)(2,1)}, u32[]{:S(2)}, u32[]{:S(2)}) %collective-permute-start.4) | collective-permute-done | bytes 1835040 | tf_op jit(solution)/shard_map/ppermute | solution.py:265
  281.2 8.2 %shard_map.41.rest_8_ = f32[2,16,256,1024]{3,2,1,0:T(8,128)} custom-call(s32[1]{0:T(128)} %bitcast.me_ref, bf16[8,16,2,32,128]{4,3,2,1,0:T(8,128)(2,1)S(1)} %all-to-all-done.rest_0_, bf16[8,16,2,32,128]{4,3,2,1,0:T(8,128)(2,1)} %collective-permute-done.6.rest_1_, ...), custom_call_target="tpu_custom_call", output_to_operand_aliasing={{}: (9, {})} | custom-call | flops 4294967296 | bytes 12582912 | tf_op jit(solution)/shard_map/pallas_call | solution.py:220
  289.4 28.3 %collective-permute-done.13.rest_6_ = bf16[8,2,2,32,896]{4,3,2,1,0:T(8,128)(2,1)} collective-permute-done((bf16[8,2,2,32,896]{4,3,2,1,0:T(8,128)(2,1)}, bf16[8,2,2,32,896]{4,3,2,1,0:T(8,128)(2,1)}, u32[]{:S(2)}, u32[]{:S(2)}) %collective-permute-start.13) | collective-permute-done | bytes 1835040 | tf_op jit(solution)/shard_map/ppermute | solution.py:265
  330.0 8.2 %shard_map.42.rest_8_ = f32[2,16,256,1024]{3,2,1,0:T(8,128)} custom-call(s32[1]{0:T(128)} %bitcast.me_ref, bf16[8,16,2,32,128]{4,3,2,1,0:T(8,128)(2,1)S(1)} %all-to-all-done.rest_0_, bf16[8,16,2,32,128]{4,3,2,1,0:T(8,128)(2,1)} %collective-permute-done.6.rest_1_, ...), custom_call_target="tpu_custom_call", output_to_operand_aliasing={{}: (9, {})} | custom-call | flops 4294967296 | bytes 12582912 | tf_op jit(solution)/shard_map/pallas_call | solution.py:220
  338.2 26.8 %collective-permute-done.10.rest_6_ = bf16[8,2,2,32,896]{4,3,2,1,0:T(8,128)(2,1)} collective-permute-done((bf16[8,2,2,32,896]{4,3,2,1,0:T(8,128)(2,1)}, bf16[8,2,2,32,896]{4,3,2,1,0:T(8,128)(2,1)}, u32[]{:S(2)}, u32[]{:S(2)}) %collective-permute-start.10) | collective-permute-done | bytes 1835040 | tf_op jit(solution)/shard_map/ppermute | solution.py:265
  374.3 37.3 %collective-permute-done.19.rest_6_ = bf16[8,2,2,32,896]{4,3,2,1,0:T(8,128)(2,1)} collective-permute-done((bf16[8,2,2,32,896]{4,3,2,1,0:T(8,128)(2,1)}, bf16[8,2,2,32,896]{4,3,2,1,0:T(8,128)(2,1)}, u32[]{:S(2)}, u32[]{:S(2)}) %collective-permute-start.19) | collective-permute-done | bytes 1835040 | tf_op jit(solution)/shard_map/ppermute | solution.py:265
  417.9 7.9 %shard_map.43.rest_8_ = f32[2,16,256,1024]{3,2,1,0:T(8,128)} custom-call(s32[1]{0:T(128)} %bitcast.me_ref, bf16[8,16,2,32,128]{4,3,2,1,0:T(8,128)(2,1)S(1)} %all-to-all-done.rest_0_, bf16[8,16,2,32,128]{4,3,2,1,0:T(8,128)(2,1)} %collective-permute-done.6.rest_1_, ...), custom_call_target="tpu_custom_call", output_to_operand_aliasing={{}: (9, {})} | custom-call | flops 4294967296 | bytes 12582912 | tf_op jit(solution)/shard_map/pallas_call | solution.py:220
  433.7 8.2 %shard_map.44.rest_8_ = f32[2,16,256,1024]{3,2,1,0:T(8,128)} custom-call(s32[1]{0:T(128)} %bitcast.me_ref, bf16[8,16,2,32,128]{4,3,2,1,0:T(8,128)(2,1)S(1)} %all-to-all-done.rest_0_, bf16[8,16,2,32,128]{4,3,2,1,0:T(8,128)(2,1)} %collective-permute-done.6.rest_1_, ...), custom_call_target="tpu_custom_call", output_to_operand_aliasing={{}: (9, {})} | custom-call | flops 4294967296 | bytes 12582912 | tf_op jit(solution)/shard_map/pallas_call | solution.py:220
  441.9 12.5 %collective-permute-done.16.rest_6_ = bf16[8,2,2,32,896]{4,3,2,1,0:T(8,128)(2,1)} collective-permute-done((bf16[8,2,2,32,896]{4,3,2,1,0:T(8,128)(2,1)}, bf16[8,2,2,32,896]{4,3,2,1,0:T(8,128)(2,1)}, u32[]{:S(2)}, u32[]{:S(2)}) %collective-permute-start.16) | collective-permute-done | bytes 1835040 | tf_op jit(solution)/shard_map/ppermute | solution.py:265
  455.3 6.0 %all-to-all-start.8 = ((bf16[8,1,2,32,896]{4,3,2,1,0:T(8,128)(2,1)}), bf16[8,1,2,32,896]{4,3,2,1,0:T(8,128)(2,1)S(1)}, u32[]{:S(2)}, u32[]{:S(2)}) async-start(bf16[8,1,2,32,896]{4,3,2,1,0:T(8,128)(2,1)} %get-tuple-element.67), calls=%async_computation.8 | async-start | bytes 1835008 | tf_op jit(solution)/shard_map/all_to_all | solution.py:291
  462.2 22.3 %collective-permute-done.26.rest_6_ = bf16[8,1,2,32,896]{4,3,2,1,0:T(8,128)(2,1)} collective-permute-done((bf16[8,1,2,32,896]{4,3,2,1,0:T(8,128)(2,1)}, bf16[8,1,2,32,896]{4,3,2,1,0:T(8,128)(2,1)}, u32[]{:S(2)}, u32[]{:S(2)}) %collective-permute-start.26) | collective-permute-done | bytes 917536 | tf_op jit(solution)/shard_map/ppermute | solution.py:265
  487.1 8.4 %shard_map.45.rest_8_ = f32[2,16,256,1024]{3,2,1,0:T(8,128)} custom-call(s32[1]{0:T(128)} %bitcast.me_ref, bf16[8,16,2,32,128]{4,3,2,1,0:T(8,128)(2,1)S(1)} %all-to-all-done.rest_0_, bf16[8,16,2,32,128]{4,3,2,1,0:T(8,128)(2,1)} %collective-permute-done.6.rest_1_, ...), custom_call_target="tpu_custom_call", output_to_operand_aliasing={{}: (9, {})} | custom-call | flops 4294967296 | bytes 12582912 | tf_op jit(solution)/shard_map/pallas_call | solution.py:220
  495.6 8.5 %shard_map.46.rest_8_ = f32[2,16,256,1024]{3,2,1,0:T(8,128)} custom-call(s32[1]{0:T(128)} %bitcast.me_ref, bf16[8,16,2,32,128]{4,3,2,1,0:T(8,128)(2,1)S(1)} %all-to-all-done.rest_0_, bf16[8,16,2,32,128]{4,3,2,1,0:T(8,128)(2,1)} %collective-permute-done.6.rest_1_, ...), custom_call_target="tpu_custom_call", output_to_operand_aliasing={{}: (9, {})} | custom-call | flops 4294967296 | bytes 12582912 | tf_op jit(solution)/shard_map/pallas_call | solution.py:220
  (123 shorter events, 88.3 us)
Async XLA Ops:
  14.1 55.7 %all-to-all-start = ((bf16[8,16,2,32,128]{4,3,2,1,0:T(8,128)(2,1)}), bf16[8,16,2,32,128]{4,3,2,1,0:T(8,128)(2,1)S(1)}, u32[]{:S(2)}, u32[]{:S(2)}) async-start(bf16[8,16,2,32,128]{4,3,2,1,0:T(8,128)(2,1)} %shard_map.37), calls=%async_computation | async-start | bytes 4194304 | tf_op jit(solution)/shard_map/all_to_all | solution.py:291
  69.8 52.7 %all-to-all-start.1 = ((bf16[8,2,2,32,896]{4,3,2,1,0:T(8,128)(2,1)}), bf16[8,2,2,32,896]{4,3,2,1,0:T(8,128)(2,1)}, u32[]{:S(2)}, u32[]{:S(2)}) async-start(bf16[8,2,2,32,896]{4,3,2,1,0:T(8,128)(2,1)} %get-tuple-element.47), calls=%async_computation.1 | async-start | bytes 3670016 | tf_op jit(solution)/shard_map/all_to_all | solution.py:291
  74.2 48.3 %collective-permute-start = (bf16[8,16,2,32,128]{4,3,2,1,0:T(8,128)(2,1)S(1)}, bf16[8,16,2,32,128]{4,3,2,1,0:T(8,128)(2,1)}, u32[]{:S(2)}, u32[]{:S(2)}) collective-permute-start(bf16[8,16,2,32,128]{4,3,2,1,0:T(8,128)(2,1)S(1)} %all-to-all-done.rest_0_), channel_id=1, source_target_pairs={{0,2},{1,3},{2,0},{3,1},{4,6},{5,7},{6,4},{7,5},{8,10},{9,11},{10,... | collective-permute-start | bytes 6291464 | tf_op jit(solution)/shard_map/ppermute | solution.py:265
  75.7 46.8 %collective-permute-start.6 = (bf16[8,16,2,32,128]{4,3,2,1,0:T(8,128)(2,1)S(1)}, bf16[8,16,2,32,128]{4,3,2,1,0:T(8,128)(2,1)}, u32[]{:S(2)}, u32[]{:S(2)}) collective-permute-start(bf16[8,16,2,32,128]{4,3,2,1,0:T(8,128)(2,1)S(1)} %all-to-all-done.rest_0_), channel_id=1, source_target_pairs={{0,1},{1,0},{2,3},{3,2},{4,5},{5,4},{6,7},{7,6},{8,9},{9,8},{10,11... | collective-permute-start | bytes 6291464 | tf_op jit(solution)/shard_map/ppermute | solution.py:265
  122.5 52.4 %all-to-all-start.3 = ((bf16[8,2,2,32,896]{4,3,2,1,0:T(8,128)(2,1)}), bf16[8,2,2,32,896]{4,3,2,1,0:T(8,128)(2,1)}, u32[]{:S(2)}, u32[]{:S(2)}) async-start(bf16[8,2,2,32,896]{4,3,2,1,0:T(8,128)(2,1)} %get-tuple-element.52), calls=%async_computation.3 | async-start | bytes 3670016 | tf_op jit(solution)/shard_map/all_to_all | solution.py:291
  128.4 45.2 %collective-permute-start.1 = (bf16[8,16,2,32,128]{4,3,2,1,0:T(8,128)(2,1)}, bf16[8,16,2,32,128]{4,3,2,1,0:T(8,128)(2,1)S(1)}, u32[]{:S(2)}, u32[]{:S(2)}) collective-permute-start(bf16[8,16,2,32,128]{4,3,2,1,0:T(8,128)(2,1)} %collective-permute-done.rest_2_.rest_1_), channel_id=1, source_target_pairs={{0,1},{1,0},{2,3},{3,2},{4,5},{5,4},{6,7},{7,6},{8,9},{9,8},{10,11... | collective-permute-start | bytes 6291464 | tf_op jit(solution)/shard_map/ppermute | solution.py:265
  128.6 42.4 %collective-permute-start.2 = (bf16[8,2,2,32,896]{4,3,2,1,0:T(8,128)(2,1)}, bf16[8,2,2,32,896]{4,3,2,1,0:T(8,128)(2,1)S(1)}, u32[]{:S(2)}, u32[]{:S(2)}) collective-permute-start(bf16[8,2,2,32,896]{4,3,2,1,0:T(8,128)(2,1)} %all-to-all-done.1.rest_4_), channel_id=1, source_target_pairs={{0,2},{1,3},{2,0},{3,1},{4,6},{5,7},{6,4},{7,5},{8,10},{9,11},{10,... | collective-permute-start | bytes 5505032 | tf_op jit(solution)/shard_map/ppermute | solution.py:265
  129.1 43.2 %collective-permute-start.3 = (bf16[8,2,2,32,896]{4,3,2,1,0:T(8,128)(2,1)}, bf16[8,2,2,32,896]{4,3,2,1,0:T(8,128)(2,1)S(1)}, u32[]{:S(2)}, u32[]{:S(2)}) collective-permute-start(bf16[8,2,2,32,896]{4,3,2,1,0:T(8,128)(2,1)} %all-to-all-done.1.rest_4_), channel_id=1, source_target_pairs={{0,1},{1,0},{2,3},{3,2},{4,5},{5,4},{6,7},{7,6},{8,9},{9,8},{10,11... | collective-permute-start | bytes 5505032 | tf_op jit(solution)/shard_map/ppermute | solution.py:265
  174.9 50.1 %all-to-all-start.2 = ((bf16[8,2,2,32,896]{4,3,2,1,0:T(8,128)(2,1)}), bf16[8,2,2,32,896]{4,3,2,1,0:T(8,128)(2,1)}, u32[]{:S(2)}, u32[]{:S(2)}) async-start(bf16[8,2,2,32,896]{4,3,2,1,0:T(8,128)(2,1)} %get-tuple-element.49), calls=%async_computation.2 | async-start | bytes 3670016 | tf_op jit(solution)/shard_map/all_to_all | solution.py:291
  180.9 41.7 %collective-permute-start.7 = (bf16[8,2,2,32,896]{4,3,2,1,0:T(8,128)(2,1)}, bf16[8,2,2,32,896]{4,3,2,1,0:T(8,128)(2,1)}, u32[]{:S(2)}, u32[]{:S(2)}) collective-permute-start(bf16[8,2,2,32,896]{4,3,2,1,0:T(8,128)(2,1)} %all-to-all-done.3.rest_4_), channel_id=1, source_target_pairs={{0,2},{1,3},{2,0},{3,1},{4,6},{5,7},{6,4},{7,5},{8,10},{9,11},{10,... | collective-permute-start | bytes 5505032 | tf_op jit(solution)/shard_map/ppermute | solution.py:265
  181.4 41.2 %collective-permute-start.12 = (bf16[8,2,2,32,896]{4,3,2,1,0:T(8,128)(2,1)}, bf16[8,2,2,32,896]{4,3,2,1,0:T(8,128)(2,1)S(1)}, u32[]{:S(2)}, u32[]{:S(2)}) collective-permute-start(bf16[8,2,2,32,896]{4,3,2,1,0:T(8,128)(2,1)} %all-to-all-done.3.rest_4_), channel_id=1, source_target_pairs={{0,1},{1,0},{2,3},{3,2},{4,5},{5,4},{6,7},{7,6},{8,9},{9,8},{10,11... | collective-permute-start | bytes 5505032 | tf_op jit(solution)/shard_map/ppermute | solution.py:265
  181.4 42.4 %collective-permute-start.9 = (bf16[8,2,2,32,896]{4,3,2,1,0:T(8,128)(2,1)}, bf16[8,2,2,32,896]{4,3,2,1,0:T(8,128)(2,1)S(1)}, u32[]{:S(2)}, u32[]{:S(2)}) collective-permute-start(bf16[8,2,2,32,896]{4,3,2,1,0:T(8,128)(2,1)} %copy-done.15), channel_id=1, source_target_pairs={{0,1},{1,0},{2,3},{3,2},{4,5},{5,4},{6,7},{7,6},{8,9},{9,8},{10,11... | collective-permute-start | bytes 5505032 | tf_op jit(solution)/shard_map/ppermute | solution.py:265
  225.1 47.3 %all-to-all-start.5 = ((bf16[8,2,2,32,896]{4,3,2,1,0:T(8,128)(2,1)}), bf16[8,2,2,32,896]{4,3,2,1,0:T(8,128)(2,1)}, u32[]{:S(2)}, u32[]{:S(2)}) async-start(bf16[8,2,2,32,896]{4,3,2,1,0:T(8,128)(2,1)} %get-tuple-element.58), calls=%async_computation.5 | async-start | bytes 3670016 | tf_op jit(solution)/shard_map/all_to_all | solution.py:291
  272.3 47.9 %all-to-all-start.4 = ((bf16[8,2,2,32,896]{4,3,2,1,0:T(8,128)(2,1)}), bf16[8,2,2,32,896]{4,3,2,1,0:T(8,128)(2,1)}, u32[]{:S(2)}, u32[]{:S(2)}) async-start(bf16[8,2,2,32,896]{4,3,2,1,0:T(8,128)(2,1)} %get-tuple-element.54), calls=%async_computation.4 | async-start | bytes 3670016 | tf_op jit(solution)/shard_map/all_to_all | solution.py:291
  277.1 40.6 %collective-permute-start.13 = (bf16[8,2,2,32,896]{4,3,2,1,0:T(8,128)(2,1)}, bf16[8,2,2,32,896]{4,3,2,1,0:T(8,128)(2,1)}, u32[]{:S(2)}, u32[]{:S(2)}) collective-permute-start(bf16[8,2,2,32,896]{4,3,2,1,0:T(8,128)(2,1)} %all-to-all-done.5.rest_4_), channel_id=1, source_target_pairs={{0,2},{1,3},{2,0},{3,1},{4,6},{5,7},{6,4},{7,5},{8,10},{9,11},{10,... | collective-permute-start | bytes 5505032 | tf_op jit(solution)/shard_map/ppermute | solution.py:265
  277.6 41.4 %collective-permute-start.15 = (bf16[8,2,2,32,896]{4,3,2,1,0:T(8,128)(2,1)}, bf16[8,2,2,32,896]{4,3,2,1,0:T(8,128)(2,1)S(1)}, u32[]{:S(2)}, u32[]{:S(2)}) collective-permute-start(bf16[8,2,2,32,896]{4,3,2,1,0:T(8,128)(2,1)} %collective-permute-done.4.rest_6_), channel_id=1, source_target_pairs={{0,1},{1,0},{2,3},{3,2},{4,5},{5,4},{6,7},{7,6},{8,9},{9,8},{10,11... | collective-permute-start | bytes 5505032 | tf_op jit(solution)/shard_map/ppermute | solution.py:265
  320.2 47.4 %all-to-all-start.7 = ((bf16[8,2,2,32,896]{4,3,2,1,0:T(8,128)(2,1)}), bf16[8,2,2,32,896]{4,3,2,1,0:T(8,128)(2,1)}, u32[]{:S(2)}, u32[]{:S(2)}) async-start(bf16[8,2,2,32,896]{4,3,2,1,0:T(8,128)(2,1)} %get-tuple-element.65), calls=%async_computation.7 | async-start | bytes 3670016 | tf_op jit(solution)/shard_map/all_to_all | solution.py:291
  367.6 45.2 %all-to-all-start.6 = ((bf16[8,2,2,32,896]{4,3,2,1,0:T(8,128)(2,1)}), bf16[8,2,2,32,896]{4,3,2,1,0:T(8,128)(2,1)}, u32[]{:S(2)}, u32[]{:S(2)}) async-start(bf16[8,2,2,32,896]{4,3,2,1,0:T(8,128)(2,1)} %get-tuple-element.60), calls=%async_computation.6 | async-start | bytes 3670016 | tf_op jit(solution)/shard_map/all_to_all | solution.py:291
  373.8 52.0 %collective-permute-start.24 = (bf16[8,2,2,32,896]{4,3,2,1,0:T(8,128)(2,1)}, bf16[8,2,2,32,896]{4,3,2,1,0:T(8,128)(2,1)}, u32[]{:S(2)}, u32[]{:S(2)}) collective-permute-start(bf16[8,2,2,32,896]{4,3,2,1,0:T(8,128)(2,1)} %all-to-all-done.7.rest_4_), channel_id=1, source_target_pairs={{0,1},{1,0},{2,3},{3,2},{4,5},{5,4},{6,7},{7,6},{8,9},{9,8},{10,11... | collective-permute-start | bytes 5505032 | tf_op jit(solution)/shard_map/ppermute | solution.py:265
  373.8 52.0 %collective-permute-start.21 = (bf16[8,2,2,32,896]{4,3,2,1,0:T(8,128)(2,1)}, bf16[8,2,2,32,896]{4,3,2,1,0:T(8,128)(2,1)}, u32[]{:S(2)}, u32[]{:S(2)}) collective-permute-start(bf16[8,2,2,32,896]{4,3,2,1,0:T(8,128)(2,1)} %collective-permute-done.10.rest_6_), channel_id=1, source_target_pairs={{0,1},{1,0},{2,3},{3,2},{4,5},{5,4},{6,7},{7,6},{8,9},{9,8},{10,11... | collective-permute-start | bytes 5505032 | tf_op jit(solution)/shard_map/ppermute | solution.py:265
  411.6 42.8 %collective-permute-start.20 = (bf16[8,2,2,32,896]{4,3,2,1,0:T(8,128)(2,1)}, bf16[8,2,2,32,896]{4,3,2,1,0:T(8,128)(2,1)}, u32[]{:S(2)}, u32[]{:S(2)}) collective-permute-start(bf16[8,2,2,32,896]{4,3,2,1,0:T(8,128)(2,1)} %collective-permute-done.19.rest_6_), channel_id=1, source_target_pairs={{0,1},{1,0},{2,3},{3,2},{4,5},{5,4},{6,7},{7,6},{8,9},{9,8},{10,11... | collective-permute-start | bytes 5505032 | tf_op jit(solution)/shard_map/ppermute | solution.py:265
  412.8 41.6 %collective-permute-start.16 = (bf16[8,2,2,32,896]{4,3,2,1,0:T(8,128)(2,1)}, bf16[8,2,2,32,896]{4,3,2,1,0:T(8,128)(2,1)}, u32[]{:S(2)}, u32[]{:S(2)}) collective-permute-start(bf16[8,2,2,32,896]{4,3,2,1,0:T(8,128)(2,1)} %all-to-all-done.6.rest_4_), channel_id=1, source_target_pairs={{0,2},{1,3},{2,0},{3,1},{4,6},{5,7},{6,4},{7,5},{8,10},{9,11},{10,... | collective-permute-start | bytes 5505032 | tf_op jit(solution)/shard_map/ppermute | solution.py:265
  413.3 41.1 %collective-permute-start.17 = (bf16[8,2,2,32,896]{4,3,2,1,0:T(8,128)(2,1)}, bf16[8,2,2,32,896]{4,3,2,1,0:T(8,128)(2,1)}, u32[]{:S(2)}, u32[]{:S(2)}) collective-permute-start(bf16[8,2,2,32,896]{4,3,2,1,0:T(8,128)(2,1)} %all-to-all-done.6.rest_4_), channel_id=1, source_target_pairs={{0,1},{1,0},{2,3},{3,2},{4,5},{5,4},{6,7},{7,6},{8,9},{9,8},{10,11... | collective-permute-start | bytes 5505032 | tf_op jit(solution)/shard_map/ppermute | solution.py:265
  462.0 42.1 %collective-permute-start.25 = (bf16[8,1,2,32,896]{4,3,2,1,0:T(8,128)(2,1)}, bf16[8,1,2,32,896]{4,3,2,1,0:T(8,128)(2,1)}, u32[]{:S(2)}, u32[]{:S(2)}) collective-permute-start(bf16[8,1,2,32,896]{4,3,2,1,0:T(8,128)(2,1)} %copy-done.7), channel_id=1, source_target_pairs={{0,1},{1,0},{2,3},{3,2},{4,5},{5,4},{6,7},{7,6},{8,9},{9,8},{10,11... | collective-permute-start | bytes 2752520 | tf_op jit(solution)/shard_map/ppermute | solution.py:265
  (41 other events, 548.5 us)
